TPU v7x, 32 devices: a whole 2x2x4 slice. The times are simulated.
32 devices in a mesh: parts: 2 (over y), gx: 4 (over z), gy: 2 (over x), gz: 2 (over core).
Axes of the slice: x: 2, y: 2, z: 4, core: 2. Of those that a mesh axis runs over, the one named last changes fastest.
Arguments:
- species: int32 [2048], P(('parts', 'gx', 'gy', 'gz')), parts along dimension 0, may hold values from 0 to 1
- send_x: int32 [32, 2, 176], P(('parts', 'gx', 'gy', 'gz')), parts along dimension 0, may hold values from 0 to 295, as said below
- send_y: int32 [32, 2, 80], P(('parts', 'gx', 'gy', 'gz')), parts along dimension 0, may hold values from 0 to 135, as said below
- send_z: int32 [32, 2, 36], P(('parts', 'gx', 'gy', 'gz')), parts along dimension 0, may hold values from 0 to 63, as said below
- edge_first: int32 [32, 1280], P(('parts', 'gx', 'gy', 'gz')), parts along dimension 0, may hold values from 0 to 63
- edge_second: int32 [32, 1280], P(('parts', 'gx', 'gy', 'gz')), parts along dimension 0, may hold values from 0 to 647, as said below
- edge_live: int32 [32, 1280], P(('parts', 'gx', 'gy', 'gz')), parts along dimension 0, may hold values from 0 to 1, as said below
- edge_vec: float32 [3, 40960], P(None, ('parts', 'gx', 'gy', 'gz')), parts along dimension 1, may hold values from -4.9 to 4.9, as said below
- embed: float32 [2, 128], replicated, may hold values from -6 to 6
- radial_in: float32 [2, 8, 64], replicated, may hold values from -6 to 6
- radial_mid: float32 [2, 64, 64], replicated, may hold values from -1.5 to 1.5
- radial_out: float32 [2, 64, 384], replicated, may hold values from -1.5 to 1.5
- mix: float32 [2, 128, 128], replicated, may hold values from -0.5 to 0.5
- update: float32 [2, 384, 128], replicated, may hold values from -0.3125 to 0.3125
- readout: float32 [2, 128], replicated, may hold values from -0.5 to 0.5
Outputs:
- energies: float32 [2048], P(('parts', 'gx', 'gy', 'gz')), parts along dimension 0
- forces: float32 [3, 2048], P(None, ('parts', 'gx', 'gy', 'gz')), parts along dimension 1
There are 2 independent parts, one for each index of `parts`. A program takes and returns all parts, laid end to end along the dimension named above; an argument that names none is the same for every part. Nothing has to cross between parts.
Inputs may be any that keep to these rules, and one draw needn't show every extreme that they name: `send_x`: the entries of one domain and side are distinct. `send_y`: the entries of one domain and side are distinct. `send_z`: the entries of one domain and side are distinct. `edge_second`: in each domain's row the entries below 64 come first, and each of them differs from edge_first's entry. `edge_live`: each domain's row is ones then zeros, with at least 640 ones and at least as many ones as edge_second has entries below 64; some domain's row is all ones. `edge_vec`: every column has length between 1 and 4.9.
All inputs are finite; a program needn't handle non-finite values.
Results may differ from a plain program's by a relative error of at most 0.0003.
Values sent between devices are 32-bit elements; how exact they have to be, the bound alone decides.
No kernel may reach another device: no remote copies, remote signals or barrier semaphores. Data moves between devices by JAX's collectives and lax.ppermute only.
A program may use at most 64 MiB of HBM per device.

v0:
```python
import math

import jax
import jax.numpy as jnp
from jax import lax
from jax.sharding import PartitionSpec as P

EDGE_BLOCK = 256


HIGH = lax.Precision.HIGHEST
CUTOFF = 5.0
INV_COUNT = 0.2
ROOT3 = math.sqrt(3.0)
ROOT5 = math.sqrt(5.0)
ROOT15 = math.sqrt(15.0)
DEGREES = (0, 1, 1, 1, 2, 2, 2, 2, 2)


def shifted(shard, axis, by):
    peers = lax.axis_size(axis)
    return lax.ppermute(shard, axis, [(i, (i + by) % peers) for i in range(peers)])


def harmonics(vec):
    dist = jnp.sqrt(vec[0] * vec[0] + vec[1] * vec[1] + vec[2] * vec[2])
    unit_x = vec[0] / dist
    unit_y = vec[1] / dist
    unit_z = vec[2] / dist
    values = [
        jnp.ones_like(dist),
        ROOT3 * unit_x,
        ROOT3 * unit_y,
        ROOT3 * unit_z,
        ROOT15 * unit_x * unit_y,
        ROOT15 * unit_y * unit_z,
        0.5 * ROOT5 * (3.0 * unit_z * unit_z - 1.0),
        ROOT15 * unit_x * unit_z,
        0.5 * ROOT15 * (unit_x * unit_x - unit_y * unit_y),
    ]
    return (dist, values)


def radial(dist, live, radial_in, radial_mid, radial_out):
    orders = jnp.arange(1, radial_in.shape[0] + 1, dtype=jnp.float32)
    basis = (
        math.sqrt(2.0 / CUTOFF)
        * jnp.sin(orders[None, :] * (math.pi / CUTOFF) * dist[:, None])
        / dist[:, None]
    )
    scaled = dist / CUTOFF
    envelope = 1.0 - 21.0 * scaled**5 + 35.0 * scaled**6 - 15.0 * scaled**7
    hidden = jax.nn.silu(jnp.dot(basis, radial_in, precision=HIGH))
    hidden = jax.nn.silu(jnp.dot(hidden, radial_mid, precision=HIGH))
    return jnp.dot(hidden, radial_out, precision=HIGH) * (envelope * live)[:, None]


def edge_terms(feat_first, feat_second, vec, live, radial_in, radial_mid, radial_out):
    width = feat_first.shape[1]
    dist, values = harmonics(vec)
    weights = radial(dist, live, radial_in, radial_mid, radial_out)
    to_first = []
    to_second = []
    for order, degree in enumerate(DEGREES):
        factor = (
            weights[:, degree * width : (degree + 1) * width] * values[order][:, None] * INV_COUNT
        )
        parity = -1.0 if degree == 1 else 1.0
        to_first.append(factor * feat_second)
        to_second.append(parity * factor * feat_first)
    return (jnp.concatenate(to_first, axis=1), jnp.concatenate(to_second, axis=1))


def invariants(amat, width):
    count = amat.shape[0]
    vector_part = amat[:, width : 4 * width].reshape(count, 3, width)
    tensor_part = amat[:, 4 * width :].reshape(count, 5, width)
    return jnp.concatenate(
        [
            amat[:, :width],
            jnp.sum(vector_part * vector_part, axis=1),
            jnp.sum(tensor_part * tensor_part, axis=1),
        ],
        axis=1,
    )


def node_update(features, amat, update):
    preact = jnp.dot(invariants(amat, features.shape[1]), update, precision=HIGH)
    return (features + jax.nn.silu(preact), preact)


def update_back(d_features, preact, amat, update):
    width = d_features.shape[1]
    gate = jax.nn.sigmoid(preact)
    d_pre = d_features * gate * (1.0 + preact * (1.0 - gate))
    d_inv = jnp.dot(d_pre, update.T, precision=HIGH)
    return jnp.concatenate(
        [
            d_inv[:, :width],
            2.0 * amat[:, width : 4 * width] * jnp.tile(d_inv[:, width : 2 * width], (1, 3)),
            2.0 * amat[:, 4 * width :] * jnp.tile(d_inv[:, 2 * width :], (1, 5)),
        ],
        axis=1,
    )


def deliver_z(faces):
    got = [None, None]
    for offset, source, target in ((-1, 1, 0), (1, 0, 1)):
        got[target] = shifted(faces[source], "gz", offset)
    return jnp.concatenate(got, axis=0)


def deliver_y(faces):
    got = [None, None]
    for offset, source, target in ((-1, 1, 0), (1, 0, 1)):
        got[target] = shifted(faces[source], "gy", offset)
    return jnp.concatenate(got, axis=0)


def deliver_x(faces):
    got = [None, None]
    for offset, source, target in ((-1, 1, 0), (1, 0, 1)):
        got[target] = shifted(faces[source], "gx", offset)
    return jnp.concatenate(got, axis=0)


def deliveries():
    return (deliver_z, deliver_y, deliver_x)


def pull_ghosts(own_rows, lists):
    rows = own_rows
    width = own_rows.shape[1]
    for deliver, table in zip(deliveries(), lists):
        faces = rows[table.reshape(-1)].reshape(2, table.shape[1], width)
        rows = jnp.concatenate([rows, deliver(faces)], axis=0)
    return rows


def push_ghosts(ext_rows, lists):
    rows = ext_rows
    width = ext_rows.shape[1]
    for deliver, table in reversed(list(zip(deliveries(), lists))):
        size = 2 * table.shape[1]
        keep = rows.shape[0] - size
        received = deliver(rows[keep:].reshape(2, table.shape[1], width))
        rows = rows[:keep].at[table.reshape(-1)].add(received)
    return rows


def edge_pass(mixed_ext, total, first, second, edge_vec, live, params, begin, finish):

    def step(index, running):
        offset = index * EDGE_BLOCK
        first_rows = lax.dynamic_slice_in_dim(first, offset, EDGE_BLOCK)
        second_rows = lax.dynamic_slice_in_dim(second, offset, EDGE_BLOCK)
        vec_block = lax.dynamic_slice_in_dim(edge_vec, offset, EDGE_BLOCK, 1)
        live_block = lax.dynamic_slice_in_dim(live, offset, EDGE_BLOCK)
        to_first, to_second = edge_terms(
            mixed_ext[first_rows], mixed_ext[second_rows], vec_block, live_block, *params
        )
        return running.at[first_rows].add(to_first).at[second_rows].add(to_second)

    return lax.fori_loop(begin, finish, step, total)


def layer_sums(features, mixing, params, lists, first, second, edge_vec, live):
    own_count = features.shape[0]
    width = features.shape[1]
    ghost_count = sum((2 * table.shape[1] for table in lists))
    own_mixed = jnp.dot(features, mixing, precision=HIGH)
    total = jnp.zeros((own_count + ghost_count, 9 * width), jnp.float32)
    ghost_rows = pull_ghosts(features, lists)[own_count:]
    mixed_ext = jnp.concatenate([own_mixed, jnp.dot(ghost_rows, mixing, precision=HIGH)], axis=0)
    total = edge_pass(
        mixed_ext, total, first, second, edge_vec, live, params, 0, first.shape[0] // EDGE_BLOCK
    )
    return (mixed_ext, total)


def edge_back(mixed_ext, d_amat_ext, first, second, edge_vec, live, params, need_features):
    block_count = first.shape[0] // EDGE_BLOCK

    def step(index, carry):
        d_mixed, d_vec = carry
        offset = index * EDGE_BLOCK
        first_rows = lax.dynamic_slice_in_dim(first, offset, EDGE_BLOCK)
        second_rows = lax.dynamic_slice_in_dim(second, offset, EDGE_BLOCK)
        vec_block = lax.dynamic_slice_in_dim(edge_vec, offset, EDGE_BLOCK, 1)
        live_block = lax.dynamic_slice_in_dim(live, offset, EDGE_BLOCK)
        toward = (d_amat_ext[first_rows], d_amat_ext[second_rows])
        feat_first = mixed_ext[first_rows]
        feat_second = mixed_ext[second_rows]
        if need_features:

            def local(left, right, vec_in):
                return edge_terms(left, right, vec_in, live_block, *params)

            _, back = jax.vjp(local, feat_first, feat_second, vec_block)
            d_left, d_right, d_block = back(toward)
            d_mixed = d_mixed.at[first_rows].add(d_left).at[second_rows].add(d_right)
        else:

            def local_vec(vec_in):
                return edge_terms(feat_first, feat_second, vec_in, live_block, *params)

            _, back = jax.vjp(local_vec, vec_block)
            d_block = back(toward)[0]
        return (d_mixed, lax.dynamic_update_slice_in_dim(d_vec, d_block, offset, 1))

    start = (jnp.zeros_like(mixed_ext), jnp.zeros_like(edge_vec))
    return lax.fori_loop(0, block_count, step, start)


def shards(
    species,
    send_x,
    send_y,
    send_z,
    edge_first,
    edge_second,
    edge_live,
    edge_vec,
    embed,
    radial_in,
    radial_mid,
    radial_out,
    mix,
    update,
    readout,
):
    lists = (send_z[0], send_y[0], send_x[0])
    first = edge_first[0]
    second = edge_second[0]
    live_flags = edge_live[0]
    live = live_flags.astype(jnp.float32)
    own_count = species.shape[0]
    width = embed.shape[1]
    layer_count = readout.shape[0]
    kinds = jnp.arange(embed.shape[0], dtype=jnp.int32)
    features = jnp.dot(
        (species[:, None] == kinds[None, :]).astype(jnp.float32), embed, precision=HIGH
    )
    saved = []
    energies = jnp.zeros((own_count,), jnp.float32)
    for layer in range(layer_count):
        params = (radial_in[layer], radial_mid[layer], radial_out[layer])
        mixed_ext, amat_ext = layer_sums(
            features, mix[layer], params, lists, first, second, edge_vec, live
        )
        amat = push_ghosts(amat_ext, lists)
        features, preact = node_update(features, amat, update[layer])
        saved.append((mixed_ext, amat, preact))
        energies = energies + jnp.dot(features, readout[layer], precision=HIGH)
    d_features = jnp.zeros((own_count, width), jnp.float32)
    d_vec_total = jnp.zeros_like(edge_vec)
    for layer in reversed(range(layer_count)):
        mixed_ext, amat, preact = saved[layer]
        params = (radial_in[layer], radial_mid[layer], radial_out[layer])
        d_features = d_features + readout[layer][None, :]
        d_amat = update_back(d_features, preact, amat, update[layer])
        d_amat_ext = pull_ghosts(d_amat, lists)
        d_mixed_ext, d_vec = edge_back(
            mixed_ext, d_amat_ext, first, second, edge_vec, live, params, layer > 0
        )
        d_vec_total = d_vec_total + d_vec
        if layer > 0:
            d_ext = jnp.dot(d_mixed_ext, mix[layer].T, precision=HIGH)
            d_features = d_features + push_ghosts(d_ext, lists)
    ext_count = saved[0][0].shape[0]
    pulls = d_vec_total.T
    force_ext = jnp.zeros((ext_count, 3), jnp.float32).at[first].add(pulls).at[second].add(-pulls)
    forces = push_ghosts(force_ext, lists).T
    return (energies, forces)


def solution(mesh):
    return jax.shard_map(
        shards,
        mesh=mesh,
        in_specs=(
            P(("parts", "gx", "gy", "gz")),
            P(("parts", "gx", "gy", "gz"), None, None),
            P(("parts", "gx", "gy", "gz"), None, None),
            P(("parts", "gx", "gy", "gz"), None, None),
            P(("parts", "gx", "gy", "gz"), None),
            P(("parts", "gx", "gy", "gz"), None),
            P(("parts", "gx", "gy", "gz"), None),
            P(None, ("parts", "gx", "gy", "gz")),
            P(),
            P(),
            P(),
            P(),
            P(),
            P(),
            P(),
        ),
        out_specs=(P(("parts", "gx", "gy", "gz")), P(None, ("parts", "gx", "gy", "gz"))),
        check_vma=False,
    )
```

profile of v0, /device:TPU:0, one launch (start us, length us, event | category | flops | bytes accessed | tf_op | source)
XLA Modules:
  0.0 909.9 jit_solution(1224570877254298620)
XLA Ops:
  11.3 3.0 collective-permute-start.2
  19.5 3.7 collective-permute-start.4
  25.3 4.2 collective-permute-done.5
  30.5 125.3 %while.70 = (s32[]{:T(128)}, f32[648,1152]{1,0:T(8,128)S(1)}, s32[1280]{0:T(1024)}, f32[3,1280]{1,0:T(4,128)}, f32[8,64]{1,0:T(8,128)}, /*index=5*/f32[64,64]{1,...) while((s32[]{:T(128)}, f32[648,1152]{1,0:T(8,128)S(1)}, ...), condition=%wide.region_3.4_spmd, body=%wide.region_0.3_spmd.sunk | while | flops 91737880 | bytes 25905828 | solution.py:166
  46.3 4.6 scatter_fusion
  50.9 4.7 scatter_fusion.1
  71.3 4.6 scatter_fusion
  76.0 4.7 scatter_fusion.1
  96.4 4.6 scatter_fusion
  101.0 4.7 scatter_fusion.1
  121.4 4.6 scatter_fusion
  126.1 4.7 scatter_fusion.1
  146.5 4.6 scatter_fusion
  151.2 4.7 scatter_fusion.1
  156.6 3.8 collective-permute-start.6
  161.6 17.9 %collective-permute-done.7 = f32[176,1152]{1,0:T(8,128)} collective-permute-done((f32[176,1152]{1,0:T(8,128)S(1)}, f32[176,1152]{1,0:T(8,128)}, u32[]{:S(2)}, u32[]{:S(2)}) %collective-permute-start.7) | collective-permute-done | bytes 811040 | tf_op jit(solution)/shard_map/ppermute | solution.py:22
  179.5 12.0 %collective-permute-done.6 = f32[176,1152]{1,0:T(8,128)} collective-permute-done((f32[176,1152]{1,0:T(8,128)S(1)}, f32[176,1152]{1,0:T(8,128)}, u32[]{:S(2)}, u32[]{:S(2)}) %collective-permute-start.6) | collective-permute-done | bytes 811040 | tf_op jit(solution)/shard_map/ppermute | solution.py:22
  191.5 7.1 scatter_custom_fusion.6
  202.9 8.4 collective-permute-done.9
  211.3 5.0 collective-permute-done.8
  241.2 125.3 %while.71 = (s32[]{:T(128)}, f32[648,1152]{1,0:T(8,128)S(1)}, s32[1280]{0:T(1024)}, f32[3,1280]{1,0:T(4,128)}, f32[8,64]{1,0:T(8,128)}, /*index=5*/f32[64,64]{1,...) while((s32[]{:T(128)}, f32[648,1152]{1,0:T(8,128)S(1)}, ...), condition=%wide.region_12.13_spmd, body=%wide.region_9.12_spmd.sunk | while | flops 91737880 | bytes 25905828 | solution.py:166
  257.0 4.6 scatter_fusion.2
  261.6 4.7 scatter_fusion.3
  282.0 4.6 scatter_fusion.2
  286.7 4.7 scatter_fusion.3
  307.1 4.6 scatter_fusion.2
  311.7 4.7 scatter_fusion.3
  332.2 4.6 scatter_fusion.2
  336.8 4.7 scatter_fusion.3
  357.2 4.6 scatter_fusion.2
  361.9 4.7 scatter_fusion.3
  366.7 4.2 collective-permute-start.18
  372.1 17.5 %collective-permute-done.19 = f32[176,1152]{1,0:T(8,128)} collective-permute-done((f32[176,1152]{1,0:T(8,128)S(1)}, f32[176,1152]{1,0:T(8,128)}, u32[]{:S(2)}, u32[]{:S(2)}) %collective-permute-start.19) | collective-permute-done | bytes 811040 | tf_op jit(solution)/shard_map/ppermute | solution.py:22
  389.6 13.5 %collective-permute-done.18 = f32[176,1152]{1,0:T(8,128)} collective-permute-done((f32[176,1152]{1,0:T(8,128)S(1)}, f32[176,1152]{1,0:T(8,128)}, u32[]{:S(2)}, u32[]{:S(2)}) %collective-permute-start.18) | collective-permute-done | bytes 811040 | tf_op jit(solution)/shard_map/ppermute | solution.py:22
  403.2 7.1 scatter_custom_fusion.9
  414.6 8.4 collective-permute-done.21
  423.0 5.4 collective-permute-done.20
  441.3 9.4 %collective-permute-done.26 = f32[80,1152]{1,0:T(8,128)S(1)} collective-permute-done((f32[80,1152]{1,0:T(8,128)S(1)}, f32[80,1152]{1,0:T(8,128)S(1)}, u32[]{:S(2)}, u32[]{:S(2)}) %collective-permute-start.26) | collective-permute-done | bytes 368672 | tf_op jit(solution)/shard_map/ppermute | solution.py:22
  450.7 7.2 collective-permute-done.27
  465.0 19.3 %collective-permute-done.28 = f32[176,1152]{1,0:T(8,128)S(1)} collective-permute-done((f32[176,1152]{1,0:T(8,128)}, f32[176,1152]{1,0:T(8,128)S(1)}, u32[]{:S(2)}, u32[]{:S(2)}) %collective-permute-start.28) | collective-permute-done | bytes 811040 | tf_op jit(solution)/shard_map/ppermute | solution.py:22
  485.2 15.2 %collective-permute-done.29 = f32[176,1152]{1,0:T(8,128)} collective-permute-done((f32[176,1152]{1,0:T(8,128)}, f32[176,1152]{1,0:T(8,128)}, u32[]{:S(2)}, u32[]{:S(2)}) %collective-permute-start.29) | collective-permute-done | bytes 811040 | tf_op jit(solution)/shard_map/ppermute | solution.py:22
  500.4 9.2 %concatenate.163 = f32[648,1152]{1,0:T(8,128)S(1)} concatenate(f32[64,1152]{1,0:T(8,128)} %copy-done.10, f32[36,1152]{1,0:T(8,128)} %copy-done.27, f32[36,1152]{1,0:T(8,128)} %copy-done.29, f32[80,1152]{1,0:T(8,128)} %copy-done.34, f32[80,1152]{1,0:T(8,128)} %copy-done.36, f32[176,1152]{1,0:T(8,128)} %copy-done.40, f32[176,1152]{1,0:T(8,128)} %collective-permute-done.29), dimensions={0} | concatenate | bytes 5971968 | tf_op jit(solution)/shard_map/concatenate | solution.py:138
  511.0 156.1 %while.72 = (s32[]{:T(128)}, f32[648,128]{1,0:T(8,128)}, f32[3,1280]{1,0:T(4,128)}, s32[1280]{0:T(1024)}, f32[3,1280]{1,0:T(4,128)}, /*index=5*/f32[8,64]{1,0:T(...) while((s32[]{:T(128)}, f32[648,128]{1,0:T(8,128)}, ...), condition=%wide.region_32.33_spmd, body=%wide.region_18.32_spmd.sunk | while | flops 185349152 | bytes 21151292 | solution.py:214
  532.1 4.7 scatter_custom_fusion.49
  536.8 4.7 scatter_custom_fusion.50
  563.4 4.7 scatter_custom_fusion.49
  568.1 4.7 scatter_custom_fusion.50
  594.6 4.7 scatter_custom_fusion.49
  599.3 4.7 scatter_custom_fusion.50
  625.8 4.7 scatter_custom_fusion.49
  630.5 4.7 scatter_custom_fusion.50
  657.0 4.7 scatter_custom_fusion.49
  661.8 4.7 scatter_custom_fusion.50
  672.8 2.6 collective-permute-done.31
  694.5 9.4 %collective-permute-done.38 = f32[80,1152]{1,0:T(8,128)S(1)} collective-permute-done((f32[80,1152]{1,0:T(8,128)S(1)}, f32[80,1152]{1,0:T(8,128)S(1)}, u32[]{:S(2)}, u32[]{:S(2)}) %collective-permute-start.38) | collective-permute-done | bytes 368672 | tf_op jit(solution)/shard_map/ppermute | solution.py:22
  703.9 7.2 collective-permute-done.39
  715.7 2.7 collective-permute-start.40
  719.7 17.6 %collective-permute-done.40 = f32[176,1152]{1,0:T(8,128)S(1)} collective-permute-done((f32[176,1152]{1,0:T(8,128)}, f32[176,1152]{1,0:T(8,128)S(1)}, u32[]{:S(2)}, u32[]{:S(2)}) %collective-permute-start.40) | collective-permute-done | bytes 811040 | tf_op jit(solution)/shard_map/ppermute | solution.py:22
  738.2 15.6 %collective-permute-done.41 = f32[176,1152]{1,0:T(8,128)} collective-permute-done((f32[176,1152]{1,0:T(8,128)}, f32[176,1152]{1,0:T(8,128)}, u32[]{:S(2)}, u32[]{:S(2)}) %collective-permute-start.41) | collective-permute-done | bytes 811040 | tf_op jit(solution)/shard_map/ppermute | solution.py:22
  753.9 9.2 %concatenate.170 = f32[648,1152]{1,0:T(8,128)S(1)} concatenate(f32[64,1152]{1,0:T(8,128)} %copy-done.9, f32[36,1152]{1,0:T(8,128)} %copy-done.26, f32[36,1152]{1,0:T(8,128)} %copy-done.28, f32[80,1152]{1,0:T(8,128)} %copy-done.33, f32[80,1152]{1,0:T(8,128)} %copy-done.35, f32[176,1152]{1,0:T(8,128)} %copy-done.39, f32[176,1152]{1,0:T(8,128)} %collective-permute-done.41), dimensions={0} | concatenate | bytes 5971968 | tf_op jit(solution)/shard_map/concatenate | solution.py:138
  763.7 105.7 %while.73 = (s32[]{:T(128)}, f32[3,1280]{1,0:T(4,128)}, f32[3,1280]{1,0:T(4,128)}, f32[8,64]{1,0:T(8,128)}, f32[64,64]{1,0:T(8,128)}, /*index=5*/f32[64,384]{1,0...) while((s32[]{:T(128)}, f32[3,1280]{1,0:T(4,128)}, ...), condition=%wide.region_48.49_spmd, body=%wide.region_36.48_spmd.sunk | while | flops 183052064 | bytes 15699779 | solution.py:214
  870.7 9.1 scatter_custom_fusion.15
  879.9 9.3 %scatter_fusion.4 = f32[648,3]{1,0:T(8,128)S(1)} fusion(f32[648,3]{1,0:T(8,128)S(1)} %scatter_custom_fusion.15, s32[1280]{0:T(1024)S(1)} %copy-done.97, f32[1280,3]{1,0:T(8,128)S(1)} %copy.39), kind=kCustom, calls=%fused_computation.40 | custom fusion | flops 3840 | bytes 51200 | tf_op jit(solution)/shard_map/scatter-add | solution.py:274
  893.0 2.6 collective-permute-done.43
  (1468 shorter events, 494.8 us)
Async XLA Ops:
  3.0 7.5 collective-permute-start
  3.5 7.0 collective-permute-start.1
  11.3 5.0 collective-permute-start.2
  14.2 4.0 collective-permute-start.3
  19.5 5.8 collective-permute-start.4
  23.2 6.3 collective-permute-start.5
  156.6 22.9 %collective-permute-start.7 = (f32[176,1152]{1,0:T(8,128)S(1)}, f32[176,1152]{1,0:T(8,128)}, u32[]{:S(2)}, u32[]{:S(2)}) collective-permute-start(f32[176,1152]{1,0:T(8,128)S(1)} %get-tuple-element.1700), channel_id=1, source_target_pairs={{0,4},{4,8},{8,12},{12,0},{1,5},{5,9},{9,13},{13,1},{2,6},{6,10},{... | collective-permute-start | bytes 2433032 | tf_op jit(solution)/shard_map/ppermute | solution.py:22
  156.6 34.9 %collective-permute-start.6 = (f32[176,1152]{1,0:T(8,128)S(1)}, f32[176,1152]{1,0:T(8,128)}, u32[]{:S(2)}, u32[]{:S(2)}) collective-permute-start(f32[176,1152]{1,0:T(8,128)S(1)} %get-tuple-element.1699), channel_id=1, source_target_pairs={{0,12},{4,0},{8,4},{12,8},{1,13},{5,1},{9,5},{13,9},{2,14},{6,2},{... | collective-permute-start | bytes 2433032 | tf_op jit(solution)/shard_map/ppermute | solution.py:22
  199.7 11.6 %collective-permute-start.9 = (f32[80,1152]{1,0:T(8,128)S(1)}, f32[80,1152]{1,0:T(8,128)S(1)}, u32[]{:S(2)}, u32[]{:S(2)}) collective-permute-start(f32[80,1152]{1,0:T(8,128)S(1)} %get-tuple-element.1708), channel_id=1, source_target_pairs={{0,2},{2,0},{1,3},{3,1},{4,6},{6,4},{5,7},{7,5},{8,10},{10,8},{9,1... | collective-permute-start | bytes 1105928 | tf_op jit(solution)/shard_map/ppermute | solution.py:22
  200.3 16.0 %collective-permute-start.8 = (f32[80,1152]{1,0:T(8,128)S(1)}, f32[80,1152]{1,0:T(8,128)S(1)}, u32[]{:S(2)}, u32[]{:S(2)}) collective-permute-start(f32[80,1152]{1,0:T(8,128)S(1)} %get-tuple-element.1707), channel_id=1, source_target_pairs={{0,2},{2,0},{1,3},{3,1},{4,6},{6,4},{5,7},{7,5},{8,10},{10,8},{9,1... | collective-permute-start | bytes 1105928 | tf_op jit(solution)/shard_map/ppermute | solution.py:22
  218.9 1.5 collective-permute-start.11
  219.0 1.7 collective-permute-start.10
  224.1 1.3 collective-permute-start.12
  224.4 1.2 collective-permute-start.13
  226.5 4.2 collective-permute-start.14
  227.1 4.1 collective-permute-start.15
  232.4 4.9 collective-permute-start.16
  233.2 6.3 collective-permute-start.17
  366.7 23.0 %collective-permute-start.19 = (f32[176,1152]{1,0:T(8,128)S(1)}, f32[176,1152]{1,0:T(8,128)}, u32[]{:S(2)}, u32[]{:S(2)}) collective-permute-start(f32[176,1152]{1,0:T(8,128)S(1)} %get-tuple-element.1698), channel_id=1, source_target_pairs={{0,4},{4,8},{8,12},{12,0},{1,5},{5,9},{9,13},{13,1},{2,6},{6,10},{... | collective-permute-start | bytes 2433032 | tf_op jit(solution)/shard_map/ppermute | solution.py:22
  366.7 36.4 %collective-permute-start.18 = (f32[176,1152]{1,0:T(8,128)S(1)}, f32[176,1152]{1,0:T(8,128)}, u32[]{:S(2)}, u32[]{:S(2)}) collective-permute-start(f32[176,1152]{1,0:T(8,128)S(1)} %get-tuple-element.1697), channel_id=1, source_target_pairs={{0,12},{4,0},{8,4},{12,8},{1,13},{5,1},{9,5},{13,9},{2,14},{6,2},{... | collective-permute-start | bytes 2433032 | tf_op jit(solution)/shard_map/ppermute | solution.py:22
  411.4 11.6 %collective-permute-start.21 = (f32[80,1152]{1,0:T(8,128)S(1)}, f32[80,1152]{1,0:T(8,128)S(1)}, u32[]{:S(2)}, u32[]{:S(2)}) collective-permute-start(f32[80,1152]{1,0:T(8,128)S(1)} %get-tuple-element.1706), channel_id=1, source_target_pairs={{0,2},{2,0},{1,3},{3,1},{4,6},{6,4},{5,7},{7,5},{8,10},{10,8},{9,1... | collective-permute-start | bytes 1105928 | tf_op jit(solution)/shard_map/ppermute | solution.py:22
  412.6 15.8 %collective-permute-start.20 = (f32[80,1152]{1,0:T(8,128)S(1)}, f32[80,1152]{1,0:T(8,128)S(1)}, u32[]{:S(2)}, u32[]{:S(2)}) collective-permute-start(f32[80,1152]{1,0:T(8,128)S(1)} %get-tuple-element.1705), channel_id=1, source_target_pairs={{0,2},{2,0},{1,3},{3,1},{4,6},{6,4},{5,7},{7,5},{8,10},{10,8},{9,1... | collective-permute-start | bytes 1105928 | tf_op jit(solution)/shard_map/ppermute | solution.py:22
  430.9 1.5 collective-permute-start.23
  430.9 1.7 collective-permute-start.22
  435.3 22.6 %copy-start.10 = (f32[64,1152]{1,0:T(8,128)}, f32[64,1152]{1,0:T(8,128)S(1)}, u32[]{:S(2)}) copy-start(f32[64,1152]{1,0:T(8,128)S(1)} %pad_maximum_fusion.4) | copy-start | bytes 884740
  436.2 1.5 collective-permute-start.24
  436.5 1.4 collective-permute-start.25
  437.7 20.2 %copy-start.27 = (f32[36,1152]{1,0:T(8,128)}, f32[36,1152]{1,0:T(8,128)S(1)}, u32[]{:S(2)}) copy-start(f32[36,1152]{1,0:T(8,128)S(1)} %collective-permute-done.24) | copy-start | bytes 497668
  438.0 19.9 %copy-start.29 = (f32[36,1152]{1,0:T(8,128)}, f32[36,1152]{1,0:T(8,128)S(1)}, u32[]{:S(2)}) copy-start(f32[36,1152]{1,0:T(8,128)S(1)} %collective-permute-done.25) | copy-start | bytes 497668
  439.2 11.5 %collective-permute-start.26 = (f32[80,1152]{1,0:T(8,128)S(1)}, f32[80,1152]{1,0:T(8,128)S(1)}, u32[]{:S(2)}, u32[]{:S(2)}) collective-permute-start(f32[80,1152]{1,0:T(8,128)S(1)} %get-tuple-element.1712), channel_id=1, source_target_pairs={{0,2},{2,0},{1,3},{3,1},{4,6},{6,4},{5,7},{7,5},{8,10},{10,8},{9,1... | collective-permute-start | bytes 1105928 | tf_op jit(solution)/shard_map/ppermute | solution.py:22
  440.4 18.8 %copy-start.95 = (s32[1024]{0:T(1024)S(1)}, s32[1024]{0:T(1024)}, u32[]{:S(2)}) copy-start(s32[1024]{0:T(1024)} %copy-done.93) | copy-start | bytes 12292
  440.4 17.5 %collective-permute-start.27 = (f32[80,1152]{1,0:T(8,128)S(1)}, f32[80,1152]{1,0:T(8,128)S(1)}, u32[]{:S(2)}, u32[]{:S(2)}) collective-permute-start(f32[80,1152]{1,0:T(8,128)S(1)} %get-tuple-element.1711), channel_id=1, source_target_pairs={{0,2},{2,0},{1,3},{3,1},{4,6},{6,4},{5,7},{7,5},{8,10},{10,8},{9,1... | collective-permute-start | bytes 1105928 | tf_op jit(solution)/shard_map/ppermute | solution.py:22
  462.4 21.8 %collective-permute-start.28 = (f32[176,1152]{1,0:T(8,128)}, f32[176,1152]{1,0:T(8,128)S(1)}, u32[]{:S(2)}, u32[]{:S(2)}) collective-permute-start(f32[176,1152]{1,0:T(8,128)} %get-tuple-element.1704), channel_id=1, source_target_pairs={{0,12},{4,0},{8,4},{12,8},{1,13},{5,1},{9,5},{13,9},{2,14},{6,2},{... | collective-permute-start | bytes 2433032 | tf_op jit(solution)/shard_map/ppermute | solution.py:22
  463.4 37.0 %collective-permute-start.29 = (f32[176,1152]{1,0:T(8,128)}, f32[176,1152]{1,0:T(8,128)}, u32[]{:S(2)}, u32[]{:S(2)}) collective-permute-start(f32[176,1152]{1,0:T(8,128)} %get-tuple-element.1703), channel_id=1, source_target_pairs={{0,4},{4,8},{8,12},{12,0},{1,5},{5,9},{9,13},{13,1},{2,6},{6,10},{... | collective-permute-start | bytes 2433032 | tf_op jit(solution)/shard_map/ppermute | solution.py:22
  667.1 20.8 %copy-start.32 = (f32[2,384,128]{2,1,0:T(8,128)S(1)}, f32[2,384,128]{2,1,0:T(8,128)}, u32[]{:S(2)}) copy-start(f32[2,384,128]{2,1,0:T(8,128)} %param.36) | copy-start | bytes 1179652
  667.1 20.8 %copy-start.69 = (f32[64,128]{1,0:T(8,128)S(1)}, f32[64,128]{1,0:T(8,128)}, u32[]{:S(2)}) copy-start(f32[64,128]{1,0:T(8,128)} %get-tuple-element.1760) | copy-start | bytes 98308
  668.9 19.5 %copy-start.25 = (f32[64,1152]{1,0:T(8,128)S(1)}, f32[64,1152]{1,0:T(8,128)}, u32[]{:S(2)}) copy-start(f32[64,1152]{1,0:T(8,128)} %copy-done.24) | copy-start | bytes 884740
  668.9 6.5 collective-permute-start.31
  671.3 5.0 collective-permute-start.30
  678.9 4.1 collective-permute-start.33
  679.6 4.0 collective-permute-start.32
  685.2 1.3 collective-permute-start.35
  685.3 1.3 collective-permute-start.34
  688.5 22.7 %copy-start.9 = (f32[64,1152]{1,0:T(8,128)}, f32[64,1152]{1,0:T(8,128)S(1)}, u32[]{:S(2)}) copy-start(f32[64,1152]{1,0:T(8,128)S(1)} %pad_maximum_fusion.5) | copy-start | bytes 884740
  689.4 1.5 collective-permute-start.36
  689.8 1.4 collective-permute-start.37
  690.9 20.3 %copy-start.26 = (f32[36,1152]{1,0:T(8,128)}, f32[36,1152]{1,0:T(8,128)S(1)}, u32[]{:S(2)}) copy-start(f32[36,1152]{1,0:T(8,128)S(1)} %collective-permute-done.36) | copy-start | bytes 497668
  691.2 19.9 %copy-start.28 = (f32[36,1152]{1,0:T(8,128)}, f32[36,1152]{1,0:T(8,128)S(1)}, u32[]{:S(2)}) copy-start(f32[36,1152]{1,0:T(8,128)S(1)} %collective-permute-done.37) | copy-start | bytes 497668
  692.4 11.5 %collective-permute-start.38 = (f32[80,1152]{1,0:T(8,128)S(1)}, f32[80,1152]{1,0:T(8,128)S(1)}, u32[]{:S(2)}, u32[]{:S(2)}) collective-permute-start(f32[80,1152]{1,0:T(8,128)S(1)} %get-tuple-element.1710), channel_id=1, source_target_pairs={{0,2},{2,0},{1,3},{3,1},{4,6},{6,4},{5,7},{7,5},{8,10},{10,8},{9,1... | collective-permute-start | bytes 1105928 | tf_op jit(solution)/shard_map/ppermute | solution.py:22
  693.9 17.2 %collective-permute-start.39 = (f32[80,1152]{1,0:T(8,128)S(1)}, f32[80,1152]{1,0:T(8,128)S(1)}, u32[]{:S(2)}, u32[]{:S(2)}) collective-permute-start(f32[80,1152]{1,0:T(8,128)S(1)} %get-tuple-element.1709), channel_id=1, source_target_pairs={{0,2},{2,0},{1,3},{3,1},{4,6},{6,4},{5,7},{7,5},{8,10},{10,8},{9,1... | collective-permute-start | bytes 1105928 | tf_op jit(solution)/shard_map/ppermute | solution.py:22
  715.7 21.6 %collective-permute-start.40 = (f32[176,1152]{1,0:T(8,128)}, f32[176,1152]{1,0:T(8,128)S(1)}, u32[]{:S(2)}, u32[]{:S(2)}) collective-permute-start(f32[176,1152]{1,0:T(8,128)} %get-tuple-element.1702), channel_id=1, source_target_pairs={{0,12},{4,0},{8,4},{12,8},{1,13},{5,1},{9,5},{13,9},{2,14},{6,2},{... | collective-permute-start | bytes 2433032 | tf_op jit(solution)/shard_map/ppermute | solution.py:22
  718.5 35.4 %collective-permute-start.41 = (f32[176,1152]{1,0:T(8,128)}, f32[176,1152]{1,0:T(8,128)}, u32[]{:S(2)}, u32[]{:S(2)}) collective-permute-start(f32[176,1152]{1,0:T(8,128)} %get-tuple-element.1701), channel_id=1, source_target_pairs={{0,4},{4,8},{8,12},{12,0},{1,5},{5,9},{9,13},{13,1},{2,6},{6,10},{... | collective-permute-start | bytes 2433032 | tf_op jit(solution)/shard_map/ppermute | solution.py:22
  719.7 44.0 %copy-start.3 = (f32[648,128]{1,0:T(8,128)S(1)}, f32[648,128]{1,0:T(8,128)}, u32[]{:S(2)}) copy-start(f32[648,128]{1,0:T(8,128)} %copy-done.2) | copy-start | bytes 995332
  719.7 44.0 %copy-start.18 = (f32[64,384]{1,0:T(8,128)S(1)}, f32[64,384]{1,0:T(8,128)}, u32[]{:S(2)}) copy-start(f32[64,384]{1,0:T(8,128)} %copy-done.17) | copy-start | bytes 294916
  870.4 30.8 %copy-start.21 = (f32[64,128]{1,0:T(8,128)S(1)}, f32[64,128]{1,0:T(8,128)}, u32[]{:S(2)}) copy-start(f32[64,128]{1,0:T(8,128)} %copy-done.20) | copy-start | bytes 98308
  870.4 30.8 %copy-start.115 = (f32[2,128]{1,0:T(2,128)S(1)}, f32[2,128]{1,0:T(2,128)}, u32[]{:S(2)}) copy-start(f32[2,128]{1,0:T(2,128)} %param.37) | copy-start | bytes 3076
  870.7 36.1 %copy-start.68 = (f32[64,128]{1,0:T(8,128)S(1)}, f32[64,128]{1,0:T(8,128)}, u32[]{:S(2)}) copy-start(f32[64,128]{1,0:T(8,128)} %copy-done.67) | copy-start | bytes 98308
  870.7 38.7 %copy-start.1 = (f32[2,128]{1,0:T(2,128)S(1)}, f32[2,128]{1,0:T(2,128)}, u32[]{:S(2)}) copy-start(f32[2,128]{1,0:T(2,128)} %param.31) | copy-start | bytes 3076
  889.2 6.5 collective-permute-start.43
  891.0 5.5 collective-permute-start.42
  899.1 4.1 collective-permute-start.45
  900.7 4.0 collective-permute-start.44
  906.3 1.3 collective-permute-start.47
  906.4 1.3 collective-permute-start.46
  (377 other events, 857.9 us)
where the time goes:
time: 927 us; the launch traced here: 910 us
  other arithmetic  374 us (40%)
  waiting for transfers between devices  224 us (24%)
  local copies, waits for them, and re-layouts  192 us (21%)
  matrix products  63.2 us (7%)
  starting transfers between devices  49.2 us (5%)
    ppermute x48, waiting for transfers between devices, shifted(): lax.ppermute(shard, axis, [(i, (i + by) % peers) for i in range(peers)])  224 us
    scatter-add x20, other arithmetic, step(): return running.at[first_rows].add(to_first).at[second_rows].add(to_second)  93 us
    mul x45, other arithmetic, edge_terms(): weights[:, degree * width:(degree + 1) * width] * values[order][:, None]  56.9 us
    ppermute x48, starting transfers between devices, shifted(): lax.ppermute(shard, axis, [(i, (i + by) % peers) for i in range(peers)])  49.2 us
    scatter-add x10, other arithmetic, step(): d_mixed = d_mixed.at[first_rows].add(d_left).at[second_rows].add(d_right)  47.2 us
    gather x20, local copies, waits for them, and re-layouts, step(): toward = (d_amat_ext[first_rows], d_amat_ext[second_rows])  45.9 us
    scatter-add x12, other arithmetic, push_ghosts(): rows = rows[:keep].at[table.reshape(-1)].add(received)  32.9 us
    while x80, other arithmetic  27.9 us
  transfers between devices with their start and end apart: 48, of which 45 were waited for; matrix products, arithmetic and copies ran while one was open for 2% of the time, Pallas kernels for 0%

commit v1 on v0

v1 whole, which is shorter than its diff:
```python
import functools
import math

import jax
import jax.numpy as jnp
from jax import lax
from jax.experimental import pallas as pl
from jax.experimental.pallas import tpu as pltpu
from jax.sharding import PartitionSpec as P

HIGH = lax.Precision.HIGHEST
CUTOFF = 5.0
INV_COUNT = 0.2
ROOT3 = math.sqrt(3.0)
ROOT5 = math.sqrt(5.0)
ROOT15 = math.sqrt(15.0)
SPANS = ((0, 1), (1, 3), (4, 5))
LANES = 128
BLOCK = 256
F32 = jnp.float32
BF16 = jnp.bfloat16
NT = (((1,), (1,)), ((), ()))
NN = (((1,), (0,)), ((), ()))


def round_up(value, unit):
    return -(-value // unit) * unit


def dot(left, right, dims=NN):
    return lax.dot_general(left, right, dims, preferred_element_type=F32)


def dot_high(left, right, dims=NN):
    return lax.dot_general(left, right, dims, preferred_element_type=F32, precision=HIGH)


def split(value):
    high = value.astype(BF16)
    return high, (value - high.astype(F32)).astype(BF16)


def split_f32(value):
    high = value.astype(BF16).astype(F32)
    return high, value - high


def stack_weights(value):
    high, low = split_f32(value)
    return jnp.concatenate([high, low, high], axis=0).T.astype(BF16)


def stack_acts(value):
    high, low = split(value)
    return jnp.concatenate([high, high, low], axis=0)


def stack_acts_f32(value):
    high, low = split_f32(value)
    return jnp.concatenate([high, high, low, jnp.zeros_like(low)], axis=0).astype(BF16)


def iota(shape, dim):
    return lax.broadcasted_iota(jnp.int32, shape, dim)


def sigmoid(value):
    return 0.5 * jnp.tanh(0.5 * value) + 0.5


def axis_steps(size):
    return (0, 1, -1) if size > 2 else tuple(range(size))


class Neighbourhood:
    def __init__(self, sizes):
        self.sizes = sizes
        self.shifts = [
            (dx, dy, dz)
            for dx in axis_steps(sizes[0])
            for dy in axis_steps(sizes[1])
            for dz in axis_steps(sizes[2])
        ]
        self.place = {
            tuple(s % n for s, n in zip(shift, sizes)): b for b, shift in enumerate(self.shifts)
        }
        self.count = len(self.shifts)

    def block(self, *shift):
        return self.place[tuple(s % n for s, n in zip(shift, self.sizes))]

    def opposite(self, block):
        return self.block(*(-s for s in self.shifts[block]))

    def pairs(self, shift):
        nx, ny, nz = self.sizes
        out = []
        for i in range(nx):
            for j in range(ny):
                for k in range(nz):
                    here = (i * ny + j) * nz + k
                    there = ((i + shift[0]) % nx * ny + (j + shift[1]) % ny) * nz + (k + shift[2]) % nz
                    out.append((here, there))
        return out

    def fetch(self, rows):
        got = [rows]
        for shift in self.shifts[1:]:
            pairs = [(there, here) for here, there in self.pairs(shift)]
            got.append(lax.ppermute(rows, ("gx", "gy", "gz"), pairs))
        return got

    def give(self, blocks):
        got = [blocks[0]]
        for block, shift in zip(blocks[1:], self.shifts[1:]):
            got.append(lax.ppermute(block, ("gx", "gy", "gz"), self.pairs(shift)))
        return got


def resolve_kernel(hood, faces, own, edges, *refs):
    count = hood.count
    tables = refs[:count]
    first_ref, second_ref, live_ref, vec_ref, own_out, sent_out, matrix = refs[count:]
    face_z, face_y, face_x = faces
    z_end = own + 2 * face_z
    y_end = z_end + 2 * face_y
    x_end = y_end + 2 * face_x
    width = tables[0].shape[1]
    lane = iota((1, width), 1)
    sub8 = iota((8, width), 0)
    payload = [table[...] for table in tables]

    def rows(block, atom):
        shape = (8, atom.shape[1])
        return jnp.where(
            iota(shape, 0) == 0, jnp.broadcast_to(block, shape), jnp.broadcast_to(atom, shape)
        )

    def z_list(dx, dy):
        plus, minus = hood.block(dx, dy, 1), hood.block(dx, dy, -1)
        in_own, in_plus = lane < own, lane < own + face_z
        atom = jnp.where(
            in_own,
            lane.astype(F32),
            jnp.where(in_plus, payload[plus], payload[minus]),
        )
        block = jnp.where(
            in_own, float(hood.block(dx, dy, 0)), jnp.where(in_plus, float(plus), float(minus))
        )
        return rows(block, atom)

    def lookup(table, index):
        depth = table.shape[1]
        hot = (iota((depth, index.shape[1]), 0) == index).astype(F32).astype(BF16)
        return dot(table.astype(BF16), hot)

    def extend(inner, sides, begin, middle, end, raw_plus, raw_minus):
        low, high = begin // LANES * LANES, round_up(end, LANES)
        spot = lane[:, low:high]
        depth = round_up(begin, LANES)
        raw = jnp.where(spot < middle, raw_plus[:, low:high], raw_minus[:, low:high])
        raw = raw.astype(jnp.int32)
        plus = lookup(sides[0][:, :depth], raw)
        minus = plus if sides[1] is sides[0] else lookup(sides[1][:, :depth], raw)
        section = jnp.where(spot < middle, plus, minus)
        if depth > low:
            head = jnp.where(spot[:, : depth - low] < begin, inner[:, low:depth], section[:, : depth - low])
            section = jnp.concatenate([head, section[:, depth - low :]], axis=1)
        return section if low == 0 else jnp.concatenate([inner[:, :low], section], axis=1)

    z_lists = {}

    def z_cached(dx, dy):
        key = hood.block(dx, dy, 0)
        if key not in z_lists:
            z_lists[key] = z_list(dx, dy)
        return z_lists[key]

    def y_list(dx):
        return extend(
            z_cached(dx, 0),
            (z_cached(dx, 1), z_cached(dx, -1)),
            z_end,
            z_end + face_y,
            y_end,
            payload[hood.block(dx, 1, 0)],
            payload[hood.block(dx, -1, 0)],
        )

    plus_list = y_list(1)
    minus_list = plus_list if hood.block(1, 0, 0) == hood.block(-1, 0, 0) else y_list(-1)
    full = extend(
        y_list(0),
        (plus_list, minus_list),
        y_end,
        y_end + face_x,
        x_end,
        payload[hood.block(1, 0, 0)],
        payload[hood.block(-1, 0, 0)],
    )
    depth = full.shape[1]

    buckets = round_up(count + 1, 8)
    kinds = jnp.concatenate(
        [table[:, x_end : x_end + own] for table in payload]
        + [jnp.zeros((buckets - count, own), F32)],
        axis=0,
    ).astype(BF16)
    before = (iota((BLOCK, BLOCK), 0) < iota((BLOCK, BLOCK), 1)).astype(F32).astype(BF16)
    chunks = range(0, edges, BLOCK)
    spread = []
    seen = jnp.zeros((buckets, 1), F32)
    lower = jnp.zeros((buckets, 1), F32)
    rank_of = []
    bucket_of = []
    for start in chunks:
        at = slice(start, start + BLOCK)
        first = first_ref[:, at]
        live = live_ref[:, at] > 0
        found = lookup(full, second_ref[:, at])
        block, atom = found[0:1], found[1:2]
        hot_block = (iota((buckets, BLOCK), 0) == block.astype(jnp.int32)).astype(F32)
        atom_hot = (iota((own, BLOCK), 0) == atom.astype(jnp.int32)).astype(F32).astype(BF16)
        first_hot = (iota((own, BLOCK), 0) == first).astype(F32).astype(BF16)
        kind_second = jnp.sum(dot(kinds, atom_hot) * hot_block, axis=0, keepdims=True)
        kind_first = dot(kinds[:16], first_hot)[0:1]
        spread.append((first.astype(F32), block, atom, kind_first, kind_second))
        live_f = live.astype(F32)
        hot_live = hot_block * live_f
        rank_of.append(dot(hot_live.astype(BF16), before) + seen)
        bucket_of.append((hot_live, live_f))
        seen = seen + jnp.sum(hot_live, axis=1, keepdims=True)
        smaller = (block.astype(jnp.int32) < iota((buckets, BLOCK), 0)).astype(F32) * live_f
        lower = lower + jnp.sum(smaller, axis=1, keepdims=True)

    meta = jnp.sum(
        jnp.where(iota((buckets, LANES), 0) == iota((buckets, LANES), 1), lower, 0.0),
        axis=0,
        keepdims=True,
    )
    sub = iota((8, BLOCK), 0)
    data = []
    for number, start in enumerate(chunks):
        at = slice(start, start + BLOCK)
        hot_live, live_f = bucket_of[number]
        spot = jnp.sum(hot_live * (rank_of[number] + lower), axis=0, keepdims=True)
        spot = jnp.where(live_f > 0.0, spot, -1.0).astype(jnp.int32)
        matrix[:, at] = (iota((edges, BLOCK), 0) == spot).astype(F32).astype(BF16)
        first, block, atom, kind_first, kind_second = spread[number]
        vec = vec_ref[:, at]
        high, rest = split_f32(vec)
        middle, low = split_f32(rest)
        pad5 = jnp.zeros((5, BLOCK), F32)
        top = jnp.concatenate([high, first, atom, block, kind_first, kind_second], axis=0)
        data.append(
            jnp.concatenate(
                [top, jnp.concatenate([middle, pad5], axis=0), jnp.concatenate([low, pad5], axis=0)],
                axis=0,
            ).astype(BF16)
        )
    data = jnp.concatenate(data, axis=1)
    for number, start in enumerate(chunks):
        at = slice(start, start + BLOCK)
        moved = dot(data, matrix[at, :], NT)
        record = moved[0:8] + moved[8:16] + moved[16:24]
        own_out[:, at] = record
        swapped = jnp.where(
            sub == 3,
            record[4:5],
            jnp.where(sub == 4, record[3:4], jnp.where(sub == 7, record[6:7], 0.0)),
        )
        sent = jnp.where(sub < 3, -record, swapped)
        if start == 0:
            head = jnp.where(sub[:, :LANES] == 6, meta, sent[:, :LANES])
            sent_out[:, :LANES] = head
            sent_out[:, LANES:BLOCK] = sent[:, LANES:]
        else:
            sent_out[:, at] = sent


def prepare_kernel(in_ref, mid_ref, out_ref, *outs):
    for layer in range(in_ref.shape[0]):
        into = in_ref[layer]
        middle = mid_ref[layer]
        last = out_ref[layer]
        in_fw, mid_fw, out_fw, in_bw, mid_bw, out_bw = (out.at[layer] for out in outs)
        high, low = split_f32(into)
        in_fw[...] = (
            jnp.concatenate([high, low, high, jnp.zeros_like(high)], axis=0).T.astype(BF16)
        )
        mid_fw[...] = stack_weights(middle)
        out_fw[...] = stack_weights(last)
        into_t = jnp.concatenate([into, jnp.zeros_like(into)], axis=0).T
        in_bw[...] = stack_weights(into_t)
        mid_bw[...] = stack_weights(middle.T)
        high, low = split(last)
        out_bw[...] = jnp.concatenate([high, low, high], axis=1)


def geometry(chunk, need_slopes):
    vec = [chunk[k : k + 1] for k in range(3)]
    dist = jnp.sqrt(vec[0] * vec[0] + vec[1] * vec[1] + vec[2] * vec[2])
    inv = 1.0 / dist
    ux, uy, uz = (v * inv for v in vec)
    values = [
        jnp.ones_like(dist),
        ROOT3 * ux,
        ROOT3 * uy,
        ROOT3 * uz,
        ROOT15 * ux * uy,
        ROOT15 * uy * uz,
        0.5 * ROOT5 * (3.0 * uz * uz - 1.0),
        ROOT15 * ux * uz,
        0.5 * ROOT15 * (ux * ux - uy * uy),
    ]
    orders = (iota((8, dist.shape[1]), 0) + 1).astype(F32) * (math.pi / CUTOFF)
    angle = orders * dist
    scale = math.sqrt(2.0 / CUTOFF) * inv
    basis = jnp.sin(angle) * scale
    x = dist * (1.0 / CUTOFF)
    x2 = x * x
    x4 = x2 * x2
    envelope = 1.0 + x4 * x * (-21.0 + x * (35.0 - 15.0 * x))
    slopes = None
    if need_slopes:
        d_basis = orders * jnp.cos(angle) * scale - basis * inv
        d_envelope = x4 * (-105.0 + x * (210.0 - 105.0 * x)) * (1.0 / CUTOFF)
        slopes = (d_basis, d_envelope)
    return inv, (ux, uy, uz), values, basis, envelope, slopes


def radial_hidden(basis, in_fw, mid_fw):
    z1 = dot(in_fw, stack_acts_f32(basis))
    gate1 = sigmoid(z1)
    z2 = dot(mid_fw, stack_acts(z1 * gate1))
    return z1, gate1, z2, sigmoid(z2)


def scaled_hots(chunk, own, values):
    target = chunk[3:4].astype(jnp.int32)
    mask = iota((own, target.shape[1]), 0) == target
    highs, lows = [], []
    for begin, size in SPANS:
        high = []
        low = []
        for m in range(begin, begin + size):
            y_high, y_low = split_f32(values[m])
            high.append(jnp.where(mask, y_high, 0.0).astype(BF16))
            low.append(jnp.where(mask, y_low, 0.0).astype(BF16))
        highs.append(jnp.concatenate(high, axis=0))
        lows.append(jnp.concatenate(low, axis=0))
    return mask, highs, lows


def other_hot(chunk, own, total):
    code = (chunk[5:6] * float(own) + chunk[4:5]).astype(jnp.int32)
    return (iota((total, code.shape[1]), 0) == code).astype(F32).astype(BF16)


def read_chunk(edges_ref, step):
    return edges_ref[:, pl.ds(pl.multiple_of(step * BLOCK, BLOCK), BLOCK)]


def kind_features(chunk, columns):
    kind = chunk[7:8]
    out = jnp.where(kind == 0.0, columns[0], 0.0)
    for index in range(1, len(columns)):
        out = out + jnp.where(kind == float(index), columns[index], 0.0)
    return out


def collect(amat, chunk, feat, values, envelope, hidden, out_fw, own):
    z2, gate2 = hidden
    width = feat.shape[0]
    units = z2 * gate2 * (INV_COUNT * envelope)
    weights = dot(out_fw, stack_acts(units))
    _, highs, lows = scaled_hots(chunk, own, values)
    for degree, (begin, size) in enumerate(SPANS):
        high, low = split(weights[degree * width : (degree + 1) * width] * feat)
        left = jnp.concatenate([highs[degree], lows[degree], highs[degree]], axis=1)
        right = jnp.concatenate([high, high, low], axis=1)
        at = slice(begin * own, (begin + size) * own)
        amat[at, :] += dot(left, right, NT)


def node_forward(amat, features, update, own):
    parts = [amat[m * own : (m + 1) * own, :] for m in range(9)]
    inv1 = sum(p * p for p in parts[1:4])
    inv2 = sum(p * p for p in parts[4:9])
    preact = dot_high(jnp.concatenate([parts[0], inv1, inv2], axis=1), update)
    return features + preact * sigmoid(preact), preact


def node_back(amat, d_features, preact, update, own, d_amat, turned):
    width = d_features.shape[1]
    gate = sigmoid(preact)
    d_pre = d_features * gate * (1.0 + preact * (1.0 - gate))
    d_inv = dot_high(d_pre, update, NT)
    for degree, (begin, size) in enumerate(SPANS):
        rows = []
        for m in range(begin, begin + size):
            value = d_inv[:, degree * width : (degree + 1) * width]
            if degree > 0:
                value = 2.0 * amat[m * own : (m + 1) * own, :] * value
            rows.append(value)
        rows = jnp.concatenate(rows, axis=0)
        high, low = split(rows)
        d_amat[begin * own : (begin + size) * own, :] = jnp.concatenate([high, low, high], axis=1)
        turned[degree][...] = stack_weights(rows)


def edge_backward(chunk, feat, own, in_fw, mid_fw, out_fw, in_bw, mid_bw, out_bw, d_amat, turned):
    width = feat.shape[0]
    inv, unit, values, basis, envelope, (d_basis, d_envelope) = geometry(chunk, True)
    z1, gate1, z2, gate2 = radial_hidden(basis, in_fw, mid_fw)
    scale = INV_COUNT * envelope
    units = z2 * gate2
    weights = dot(out_fw, stack_acts(units * scale))
    mask, highs, lows = scaled_hots(chunk, own, values)
    pulled = []
    d_mixed = 0.0
    d_values = []
    for degree, (begin, size) in enumerate(SPANS):
        weight = weights[degree * width : (degree + 1) * width]
        right = jnp.concatenate([highs[degree], highs[degree], lows[degree]], axis=0)
        term = dot(turned[degree][...], right)
        d_mixed = d_mixed + weight * term
        pulled.append(feat * term)
        high, low = split(weight * feat)
        spread = dot(
            d_amat[begin * own : (begin + size) * own, :],
            jnp.concatenate([high, high, low], axis=0),
        )
        for m in range(size):
            d_values.append(
                jnp.sum(jnp.where(mask, spread[m * own : (m + 1) * own], 0.0), axis=0, keepdims=True)
            )
    pulled = jnp.concatenate(pulled, axis=0)
    d_units = dot(out_bw, stack_acts(pulled))
    d_env = INV_COUNT * jnp.sum(units * d_units, axis=0, keepdims=True)
    d_z2 = d_units * scale * gate2 * (1.0 + z2 * (1.0 - gate2))
    d_hidden = dot(mid_bw, stack_acts(d_z2))
    d_z1 = d_hidden * gate1 * (1.0 + z1 * (1.0 - gate1))
    d_b = dot(in_bw, stack_acts(d_z1))[0:8]
    d_dist = jnp.sum(d_b * d_basis, axis=0, keepdims=True) + d_env * d_envelope
    ux, uy, uz = unit
    y = d_values
    dux = ROOT3 * y[1] + ROOT15 * (uy * y[4] + uz * y[7] + ux * y[8])
    duy = ROOT3 * y[2] + ROOT15 * (ux * y[4] + uz * y[5] - uy * y[8])
    duz = ROOT3 * y[3] + ROOT15 * (uy * y[5] + ux * y[7]) + 3.0 * ROOT5 * uz * y[6]
    along = ux * dux + uy * duy + uz * duz
    grad = [(du - u * along) * inv + d_dist * u for u, du in zip(unit, (dux, duy, duz))]
    return grad, d_mixed


def first_kernel(hood, own, edges, *refs):
    count = hood.count
    own_rec = refs[0]
    records = refs[1 : 1 + count]
    (
        species_ref,
        embed_ref,
        mix_ref,
        update_ref,
        in_fw,
        mid_fw,
        out_fw,
        list_out,
        total_out,
        amat_out,
        preact_out,
        h_out,
        w_out,
    ) = refs[1 + count :]
    lane = iota((1, LANES), 1)
    sub = iota((8, LANES), 0)
    dummy = jnp.where(sub == 0, 1.0, jnp.where((sub >= 3) & (sub <= 5), -1.0, 0.0))
    capacity = list_out.shape[1]

    def fill(step, _):
        list_out[:, pl.ds(pl.multiple_of(step * LANES, LANES), LANES)] = dummy
        return 0

    lax.fori_loop(edges // LANES, capacity // LANES, fill, 0)

    def scalar(row, index):
        return jnp.sum(jnp.where(lane == index, row, 0.0)).astype(jnp.int32)

    filled = scalar(records[0][6:7, :LANES], count)
    for start in range(0, edges, LANES):
        at = slice(start, start + LANES)
        list_out[:, at] = jnp.where(lane + start < filled, own_rec[:, at], dummy)
    last = edges // LANES - 1
    for b in range(count):
        record = records[b]
        bucket = hood.opposite(b)
        row = record[6:7, :LANES]
        begin = scalar(row, bucket)
        size = scalar(row, bucket + 1) - begin
        to = filled

        def place(step, _, record=record, begin=begin, size=size, to=to, b=b):
            window = step * LANES - to + begin
            low = lax.shift_right_arithmetic(window, 7)
            turn = jnp.bitwise_and(window, LANES - 1)
            left = jnp.clip(low, 0, last)
            right = jnp.clip(low + 1, 0, last)
            back = jnp.bitwise_and(LANES - turn, LANES - 1)
            one = pltpu.roll(record[:, pl.ds(pl.multiple_of(left * LANES, LANES), LANES)], back, 1)
            two = pltpu.roll(record[:, pl.ds(pl.multiple_of(right * LANES, LANES), LANES)], back, 1)
            rows = jnp.where(lane < LANES - turn, one, two)
            rows = jnp.where(sub == 5, float(b), rows)
            spot = lane + step * LANES
            here = pl.ds(pl.multiple_of(step * LANES, LANES), LANES)
            list_out[:, here] = jnp.where((spot >= to) & (spot < to + size), rows, list_out[:, here])
            return 0

        lax.fori_loop(
            lax.shift_right_arithmetic(to, 7),
            lax.shift_right_arithmetic(to + size + LANES - 1, 7),
            place,
            0,
        )
        filled = to + size
    steps = lax.shift_right_arithmetic(filled + BLOCK - 1, 8)
    total_out[0] = steps

    embed = embed_ref[...]
    mixed = dot_high(embed, mix_ref[0])
    columns = [mixed[k : k + 1].T for k in range(embed.shape[0])]
    amat_out[...] = jnp.zeros_like(amat_out)

    def body(step, _):
        chunk = read_chunk(list_out, step)
        _, _, values, basis, envelope, _ = geometry(chunk, False)
        _, _, z2, gate2 = radial_hidden(basis, in_fw[0], mid_fw[0])
        feat = kind_features(chunk, columns)
        collect(amat_out, chunk, feat, values, envelope, (z2, gate2), out_fw[0], own)
        return 0

    lax.fori_loop(0, steps, body, 0)
    kind = species_ref[...]
    features = jnp.where(kind == 0, embed[0:1], 0.0)
    for k in range(1, embed.shape[0]):
        features = features + jnp.where(kind == k, embed[k : k + 1], 0.0)
    h, preact = node_forward(amat_out, features, update_ref[0], own)
    preact_out[...] = preact
    h_out[...] = h
    w_out[...] = dot_high(h, mix_ref[1])


def second_kernel(count, own, *refs):
    blocks = refs[:count]
    (
        steps_ref,
        list_ref,
        h_ref,
        update_ref,
        readout_ref,
        in_fw,
        mid_fw,
        out_fw,
        in_bw,
        mid_bw,
        out_bw,
        energy_out,
        grad_out,
    ) = refs[count : count + 13]
    d_mixed_outs = refs[count + 13 : count + 13 + count]
    features_t, amat, d_amat, turn0, turn1, turn2, d_mixed_sum = refs[count + 13 + count :]
    turned = (turn0, turn1, turn2)
    total = count * own
    width = h_ref.shape[1]
    steps = steps_ref[0]
    everyone = jnp.concatenate([block[...] for block in blocks], axis=0)
    high, low = split_f32(everyone.T)
    features_t[...] = jnp.concatenate([high, low], axis=0).astype(BF16)
    amat[...] = jnp.zeros_like(amat)
    d_mixed_sum[...] = jnp.zeros_like(d_mixed_sum)

    def gather(hot):
        both = dot(features_t[...], hot)
        return both[:width] + both[width:]

    def forward(step, _):
        chunk = read_chunk(list_ref, step)
        _, _, values, basis, envelope, _ = geometry(chunk, False)
        _, _, z2, gate2 = radial_hidden(basis, in_fw[1], mid_fw[1])
        feat = gather(other_hot(chunk, own, total))
        collect(amat, chunk, feat, values, envelope, (z2, gate2), out_fw[1], own)
        return 0

    lax.fori_loop(0, steps, forward, 0)
    h1 = h_ref[...]
    h2, preact = node_forward(amat, h1, update_ref[1], own)
    readout = readout_ref[...]
    energy_out[...] = dot_high(readout[0:1], h1, NT) + dot_high(readout[1:2], h2, NT)
    d_features = jnp.broadcast_to(readout[1:2], h1.shape)
    node_back(amat, d_features, preact, update_ref[1], own, d_amat, turned)

    def backward(step, _):
        chunk = read_chunk(list_ref, step)
        hot = other_hot(chunk, own, total)
        grad, d_mixed = edge_backward(
            chunk,
            gather(hot),
            own,
            in_fw[1],
            mid_fw[1],
            out_fw[1],
            in_bw[1],
            mid_bw[1],
            out_bw[1],
            d_amat,
            turned,
        )
        at = pl.ds(pl.multiple_of(step * BLOCK, BLOCK), BLOCK)
        grad_out[:, at] = jnp.concatenate(grad + [jnp.zeros((5, BLOCK), F32)], axis=0)
        high, low = split(d_mixed)
        both = dot(hot, jnp.concatenate([high, low], axis=0), NT)
        d_mixed_sum[...] += both[:, :width] + both[:, width:]
        return 0

    lax.fori_loop(0, steps, backward, 0)
    for b, out in enumerate(d_mixed_outs):
        out[...] = d_mixed_sum[b * own : (b + 1) * own, :]


def last_kernel(count, own, *refs):
    blocks = refs[:count]
    (
        steps_ref,
        list_ref,
        grad_ref,
        amat_ref,
        preact_ref,
        embed_ref,
        mix_ref,
        update_ref,
        readout_ref,
        in_fw,
        mid_fw,
        out_fw,
        in_bw,
        mid_bw,
        out_bw,
    ) = refs[count : count + 15]
    force_outs = refs[count + 15 : count + 15 + count]
    d_amat, turn0, turn1, turn2, force = refs[count + 15 + count :]
    turned = (turn0, turn1, turn2)
    total = count * own
    steps = steps_ref[0]
    embed = embed_ref[...]
    mixed = dot_high(embed, mix_ref[0])
    columns = [mixed[k : k + 1].T for k in range(embed.shape[0])]
    d_mixed = sum(block[...] for block in blocks)
    readout = readout_ref[...]
    d_features = readout[0:1] + readout[1:2] + dot_high(d_mixed, mix_ref[1], NT)
    node_back(amat_ref, d_features, preact_ref[...], update_ref[0], own, d_amat, turned)
    force[...] = jnp.zeros_like(force)

    def backward(step, _):
        chunk = read_chunk(list_ref, step)
        grad, _ = edge_backward(
            chunk,
            kind_features(chunk, columns),
            own,
            in_fw[0],
            mid_fw[0],
            out_fw[0],
            in_bw[0],
            mid_bw[0],
            out_bw[0],
            d_amat,
            turned,
        )
        at = pl.ds(pl.multiple_of(step * BLOCK, BLOCK), BLOCK)
        pull = jnp.concatenate(grad + [jnp.zeros((5, BLOCK), F32)], axis=0) + grad_ref[:, at]
        high, rest = split_f32(pull)
        middle, low = split_f32(rest)
        parts = jnp.concatenate([high, middle, low, jnp.zeros_like(low)], axis=0).astype(BF16)
        code = (chunk[5:6] * float(own) + chunk[4:5]).astype(jnp.int32)
        row = iota((total, BLOCK), 0)
        target = chunk[3:4].astype(jnp.int32)
        hot = (row == target).astype(F32) - (row == code).astype(F32)
        moved = dot(parts, hot.astype(BF16), NT)
        force[...] += moved[0:8] + moved[8:16] + moved[16:24]
        return 0

    lax.fori_loop(0, steps, backward, 0)
    for b, out in enumerate(force_outs):
        out[...] = force[:, b * own : (b + 1) * own]


def call(kernel, outs, scratch, args, smem_in=(), smem_out=()):
    vmem = pl.BlockSpec(memory_space=pltpu.VMEM)
    smem = pl.BlockSpec(memory_space=pltpu.SMEM)
    return pl.pallas_call(
        kernel,
        out_shape=outs,
        in_specs=[smem if k in smem_in else vmem for k in range(len(args))],
        out_specs=[smem if k in smem_out else vmem for k in range(len(outs))],
        scratch_shapes=scratch,
        compiler_params=pltpu.CompilerParams(vmem_limit_bytes=40 * 1024 * 1024),
    )(*args)


def shards(
    sizes,
    species,
    send_x,
    send_y,
    send_z,
    edge_first,
    edge_second,
    edge_live,
    edge_vec,
    embed,
    radial_in,
    radial_mid,
    radial_out,
    mix,
    update,
    readout,
):
    hood = Neighbourhood(sizes)
    count = hood.count
    own = species.shape[0]
    width = embed.shape[1]
    layers = readout.shape[0]
    hidden = radial_mid.shape[1]
    slots = edge_first.shape[1]
    edges = round_up(slots, BLOCK)
    extra = edges - slots
    if extra:
        edge_first = jnp.pad(edge_first, ((0, 0), (0, extra)))
        edge_second = jnp.pad(edge_second, ((0, 0), (0, extra)))
        edge_live = jnp.pad(edge_live, ((0, 0), (0, extra)))
        edge_vec = jnp.pad(edge_vec, ((0, 0), (0, extra)), constant_values=1.0)
    faces = tuple(send.shape[2] for send in (send_z, send_y, send_x))
    pieces = [jnp.zeros((own,), jnp.int32)]
    for send in (send_z, send_y, send_x):
        pieces += [send[0, 1], send[0, 0]]
    pieces.append(species)
    length = own * 2 + 2 * sum(faces)
    pieces.append(jnp.zeros((round_up(length, LANES) - length,), jnp.int32))
    payload = jnp.concatenate(pieces).astype(F32)[None, :]

    shape = jax.ShapeDtypeStruct
    weights = call(
        prepare_kernel,
        [
            shape((layers, hidden, 32), BF16),
            shape((layers, hidden, 3 * hidden), BF16),
            shape((layers, 3 * width, 3 * hidden), BF16),
            shape((layers, 16, 3 * hidden), BF16),
            shape((layers, hidden, 3 * hidden), BF16),
            shape((layers, hidden, 9 * width), BF16),
        ],
        [],
        [radial_in, radial_mid, radial_out],
    )
    tables = hood.fetch(payload)
    own_rec, sent = call(
        functools.partial(resolve_kernel, hood, faces, own, edges),
        [shape((8, edges), F32), shape((8, edges), F32)],
        [pltpu.VMEM((edges, edges), BF16)],
        tables + [edge_first, edge_second, edge_live, edge_vec],
    )
    records = hood.fetch(sent)
    capacity = (count + 1) * edges
    edge_list, steps, amat1, preact1, h1, w2 = call(
        functools.partial(first_kernel, hood, own, edges),
        [
            shape((8, capacity), F32),
            shape((1,), jnp.int32),
            shape((9 * own, width), F32),
            shape((own, width), F32),
            shape((own, width), F32),
            shape((own, width), F32),
        ],
        [],
        [own_rec] + records + [species[:, None], embed, mix, update] + list(weights[:3]),
        smem_out=(1,),
    )
    mixed = hood.fetch(w2)
    turned = [pltpu.VMEM((width, 3 * size * own), BF16) for _, size in SPANS]
    results = call(
        functools.partial(second_kernel, count, own),
        [shape((1, own), F32), shape((8, capacity), F32)]
        + [shape((own, width), F32)] * count,
        [
            pltpu.VMEM((2 * width, count * own), BF16),
            pltpu.VMEM((9 * own, width), F32),
            pltpu.VMEM((9 * own, 3 * width), BF16),
        ]
        + turned
        + [pltpu.VMEM((count * own, width), F32)],
        mixed + [steps, edge_list, h1, update, readout] + list(weights),
        smem_in=(count,),
    )
    energies, grads = results[:2]
    d_mixed = hood.give(list(results[2:]))
    forces = call(
        functools.partial(last_kernel, count, own),
        [shape((8, own), F32)] * count,
        [pltpu.VMEM((9 * own, 3 * width), BF16)] + turned + [pltpu.VMEM((8, count * own), F32)],
        d_mixed
        + [steps, edge_list, grads, amat1, preact1, embed, mix, update, readout]
        + list(weights),
        smem_in=(count,),
    )
    forces = sum(part[:3] for part in hood.give(list(forces)))
    return (energies.reshape(own), forces)


def solution(mesh):
    sizes = tuple(mesh.shape[axis] for axis in ("gx", "gy", "gz"))
    split_all = ("parts", "gx", "gy", "gz")
    return jax.shard_map(
        functools.partial(shards, sizes),
        mesh=mesh,
        in_specs=(
            P(split_all),
            P(split_all, None, None),
            P(split_all, None, None),
            P(split_all, None, None),
            P(split_all, None),
            P(split_all, None),
            P(split_all, None),
            P(None, split_all),
            P(),
            P(),
            P(),
            P(),
            P(),
            P(),
            P(),
        ),
        out_specs=(P(split_all), P(None, split_all)),
        check_vma=False,
    )
```

time: 927 us -> 155 us (0.17); the launches traced: 910 us -> 153 us
  other arithmetic: 374 us -> 0.6 us
  waiting for transfers between devices: 224 us -> 15 us
  local copies, waits for them, and re-layouts: 192 us -> 11.3 us
  matrix products: 63.2 us -> 0 us
  Pallas kernels: 0 us -> 54.2 us
  starting transfers between devices: 49.2 us -> 70.8 us
    ppermute x48 -> x55, waiting for transfers between devices: 224 us -> 15 us  [the longest x33 7.93 us: fetch(): got.append(lax.ppermute(rows, ('gx', 'gy', 'gz'), pairs))]
    scatter-add x44 -> x0, other arithmetic: 191 us -> none  [the longest x20 93 us: step(): return running.at[first_rows].add(to_first).at[second_rows].add(to_second)]
    gather x72 -> x0, local copies, waits for them, and re-layouts: 106 us -> none  [the longest x20 45.9 us: step(): toward = (d_amat_ext[first_rows], d_amat_ext[second_rows])]
    mul x123 -> x0, other arithmetic: 84.3 us -> none  [the longest x45 56.9 us: edge_terms(): weights[:, degree * width:(degree + 1) * width] * values[order][:, None]]
    dot_general x102 -> x0, matrix products: 63.2 us -> none  [the longest x30 25.6 us: radial(): jnp.dot(hidden, radial_out, precision=HIGH) * (envelope * live)[:, None]]
    pallas_call x0 -> x5, Pallas kernels: none -> 54.2 us  [call(): pl.pallas_call(kernel, out_shape=outs, in_specs=[smem if k in smem_in els...]
    while x80 -> x0, other arithmetic: 27.9 us -> none
    slice x59 -> x0, local copies, waits for them, and re-layouts: 27.5 us -> none  [the longest x20 17.5 us: harmonics(): dist = jnp.sqrt(vec[0] * vec[0] + vec[1] * vec[1] + vec[2] * vec[2])]
  transfers between devices with their start and end apart: 48 -> 55, of which waited for: 45 -> 13; matrix products, arithmetic and copies ran while one was open for 2% -> 0% of each run, Pallas kernels for 0% -> 0%
where the time goes in v1:
time: 155 us; the launch traced here: 153 us
  starting transfers between devices  70.8 us (46%)
  Pallas kernels  54.2 us (35%)
  waiting for transfers between devices  15 us (10%)
  local copies, waits for them, and re-layouts  11.3 us (7%)
    pallas_call x5, Pallas kernels, call(): pl.pallas_call(kernel, out_shape=outs, in_specs=[smem if k in smem_in els...  54.2 us
    ppermute x33, starting transfers between devices, fetch(): got.append(lax.ppermute(rows, ('gx', 'gy', 'gz'), pairs))  40.2 us
    ppermute x22, starting transfers between devices, give(): got.append(lax.ppermute(block, ('gx', 'gy', 'gz'), self.pairs(shift)))  30.6 us
    ppermute x33, waiting for transfers between devices, fetch(): got.append(lax.ppermute(rows, ('gx', 'gy', 'gz'), pairs))  7.93 us
    unnamed x22, local copies, waits for them, and re-layouts  7.51 us
    ppermute x22, waiting for transfers between devices, give(): got.append(lax.ppermute(block, ('gx', 'gy', 'gz'), self.pairs(shift)))  7.1 us
  transfers between devices with their start and end apart: 55, of which 13 were waited for; matrix products, arithmetic and copies ran while one was open for 0% of the time, Pallas kernels for 0%

profile of v1, /device:TPU:0, one launch (start us, length us, event | category | flops | bytes accessed | tf_op | source)
XLA Modules:
  0.0 152.8 jit_solution(3587110059029531215)
XLA Ops:
  0.6 0.8 slice_bitcast_fusion.2
  1.4 0.8 slice_bitcast_fusion.4
  2.2 0.8 slice_bitcast_fusion
  2.9 0.8 concatenate.31
  3.7 3.4 %collective-permute-start.10 = (f32[1,768]{1,0:T(1,128)S(1)}, f32[1,768]{1,0:T(1,128)S(1)}, u32[]{:S(2)}, u32[]{:S(2)}) collective-permute-start(f32[1,768]{1,0:T(1,128)S(1)} %convert_element_type.10.refs_0_), channel_id=1, source_target_pairs={{15,0},{14,1},{13,2},{12,3},{3,4},{2,5},{1,6},{0,7},{7,8},{6,9},{5... | collective-permute-start | bytes 9224 | tf_op jit(solution)/shard_map/ppermute | solution.py:110
  7.1 1.5 %collective-permute-start.9 = (f32[1,768]{1,0:T(1,128)S(1)}, f32[1,768]{1,0:T(1,128)S(1)}, u32[]{:S(2)}, u32[]{:S(2)}) collective-permute-start(f32[1,768]{1,0:T(1,128)S(1)} %convert_element_type.10.refs_0_), channel_id=1, source_target_pairs={{14,0},{15,1},{12,2},{13,3},{2,4},{3,5},{0,6},{1,7},{6,8},{7,9},{4... | collective-permute-start | bytes 9224 | tf_op jit(solution)/shard_map/ppermute | solution.py:110
  8.7 1.6 %collective-permute-start.8 = (f32[1,768]{1,0:T(1,128)S(1)}, f32[1,768]{1,0:T(1,128)S(1)}, u32[]{:S(2)}, u32[]{:S(2)}) collective-permute-start(f32[1,768]{1,0:T(1,128)S(1)} %convert_element_type.10.refs_0_), channel_id=1, source_target_pairs={{13,0},{12,1},{15,2},{14,3},{1,4},{0,5},{3,6},{2,7},{5,8},{4,9},{7... | collective-permute-start | bytes 9224 | tf_op jit(solution)/shard_map/ppermute | solution.py:110
  10.6 3.9 %collective-permute-start.6 = (f32[1,768]{1,0:T(1,128)S(1)}, f32[1,768]{1,0:T(1,128)S(1)}, u32[]{:S(2)}, u32[]{:S(2)}) collective-permute-start(f32[1,768]{1,0:T(1,128)S(1)} %convert_element_type.10.refs_0_), channel_id=1, source_target_pairs={{7,0},{6,1},{5,2},{4,3},{11,4},{10,5},{9,6},{8,7},{15,8},{14,9},{1... | collective-permute-start | bytes 9224 | tf_op jit(solution)/shard_map/ppermute | solution.py:110
  14.5 0.6 collective-permute-start.5
  15.9 1.0 collective-permute-start.2
  16.8 0.9 collective-permute-start.1
  17.7 1.3 collective-permute-done.5.refs_6_
  19.0 1.5 collective-permute-done.1.refs_2_
  20.4 0.7 copy-done.4
  21.2 0.7 copy-done.6
  21.9 0.7 copy-done.7
  22.5 0.7 copy-done.8
  23.2 2.6 %shard_map.158 = (f32[8,1280]{1,0:T(8,128)S(1)}, f32[8,1280]{1,0:T(8,128)S(1)}) custom-call(f32[1,768]{1,0:T(1,128)S(1)} %convert_element_type.10.refs_0_, f32[1,768]{1,0:T(1,128)S(1)} %collective-permute-done.refs_1_, f32[1,768]{1,0:T(1,128)S(1)} %collective-permute-done.1.refs_2_, f32[1,768]{1,0:T(1,128)S(1)} %collective-permute-done.2.refs_3_, ...), custom_call_target="tpu_custom_call" | custom-call | tf_op jit(solution)/shard_map/pallas_call | solution.py:698
  25.9 0.8 collective-permute-start.21
  26.7 2.3 %collective-permute-start.20 = (f32[8,1280]{1,0:T(8,128)S(1)}, f32[8,1280]{1,0:T(8,128)S(1)}, u32[]{:S(2)}, u32[]{:S(2)}) collective-permute-start(f32[8,1280]{1,0:T(8,128)S(1)} %get-tuple-element.43.refs_1_), channel_id=1, source_target_pairs={{14,0},{15,1},{12,2},{13,3},{2,4},{3,5},{0,6},{1,7},{6,8},{7,9},{4... | collective-permute-start | bytes 122888 | tf_op jit(solution)/shard_map/ppermute | solution.py:110
  29.0 1.8 %collective-permute-start.19 = (f32[8,1280]{1,0:T(8,128)S(1)}, f32[8,1280]{1,0:T(8,128)S(1)}, u32[]{:S(2)}, u32[]{:S(2)}) collective-permute-start(f32[8,1280]{1,0:T(8,128)S(1)} %get-tuple-element.43.refs_1_), channel_id=1, source_target_pairs={{13,0},{12,1},{15,2},{14,3},{1,4},{0,5},{3,6},{2,7},{5,8},{4,9},{7... | collective-permute-start | bytes 122888 | tf_op jit(solution)/shard_map/ppermute | solution.py:110
  31.2 2.7 %collective-permute-start.17 = (f32[8,1280]{1,0:T(8,128)S(1)}, f32[8,1280]{1,0:T(8,128)S(1)}, u32[]{:S(2)}, u32[]{:S(2)}) collective-permute-start(f32[8,1280]{1,0:T(8,128)S(1)} %get-tuple-element.43.refs_1_), channel_id=1, source_target_pairs={{7,0},{6,1},{5,2},{4,3},{11,4},{10,5},{9,6},{8,7},{15,8},{14,9},{1... | collective-permute-start | bytes 122888 | tf_op jit(solution)/shard_map/ppermute | solution.py:110
  33.9 1.3 collective-permute-start.16
  35.2 0.7 collective-permute-start.15
  36.0 0.6 collective-permute-start.14
  37.1 1.0 collective-permute-start.12
  38.0 0.9 collective-permute-done.16.refs_7_
  39.1 0.7 copy.17.refs_13_
  39.8 0.9 copy-done.2
  40.7 0.8 copy-done.3
  41.6 0.7 copy-done.5
  42.9 0.7 copy-done.10
  43.6 0.9 copy-done.1
  44.5 12.4 %shard_map.160 = (f32[8,16640]{1,0:T(8,128)S(1)}, s32[1]{0:T(128)}, f32[576,128]{1,0:T(8,128)S(1)}, f32[64,128]{1,0:T(8,128)S(1)}, f32[64,128]{1,0:T(8,128)S(1)}, /*index=5*/f32[64,128]{1,0:T(8,128)S(1)}) custom-call(f32[8,1280]{1,0:T(8,128)S(1)} %get-tuple-element.42.refs_0_, f32[8,1280]{1,0:T(8,128)S(1)} %get-tuple-element.43.refs_1_, ...), custom_call_target="tpu_custom_call" | custom-call | tf_op jit(solution)/shard_map/pallas_call | solution.py:698
  56.8 1.9 %collective-permute-start.32 = (f32[64,128]{1,0:T(8,128)S(1)}, f32[64,128]{1,0:T(8,128)S(1)}, u32[]{:S(2)}, u32[]{:S(2)}) collective-permute-start(f32[64,128]{1,0:T(8,128)S(1)} %get-tuple-element.47.refs_0_), channel_id=1, source_target_pairs={{15,0},{14,1},{13,2},{12,3},{3,4},{2,5},{1,6},{0,7},{7,8},{6,9},{5... | collective-permute-start | bytes 98312 | tf_op jit(solution)/shard_map/ppermute | solution.py:110
  58.7 3.2 %collective-permute-start.31 = (f32[64,128]{1,0:T(8,128)S(1)}, f32[64,128]{1,0:T(8,128)S(1)}, u32[]{:S(2)}, u32[]{:S(2)}) collective-permute-start(f32[64,128]{1,0:T(8,128)S(1)} %get-tuple-element.47.refs_0_), channel_id=1, source_target_pairs={{14,0},{15,1},{12,2},{13,3},{2,4},{3,5},{0,6},{1,7},{6,8},{7,9},{4... | collective-permute-start | bytes 98312 | tf_op jit(solution)/shard_map/ppermute | solution.py:110
  62.2 3.6 %collective-permute-start.28 = (f32[64,128]{1,0:T(8,128)S(1)}, f32[64,128]{1,0:T(8,128)S(1)}, u32[]{:S(2)}, u32[]{:S(2)}) collective-permute-start(f32[64,128]{1,0:T(8,128)S(1)} %get-tuple-element.47.refs_0_), channel_id=1, source_target_pairs={{7,0},{6,1},{5,2},{4,3},{11,4},{10,5},{9,6},{8,7},{15,8},{14,9},{1... | collective-permute-start | bytes 98312 | tf_op jit(solution)/shard_map/ppermute | solution.py:110
  65.8 2.3 %collective-permute-start.27 = (f32[64,128]{1,0:T(8,128)S(1)}, f32[64,128]{1,0:T(8,128)S(1)}, u32[]{:S(2)}, u32[]{:S(2)}) collective-permute-start(f32[64,128]{1,0:T(8,128)S(1)} %get-tuple-element.47.refs_0_), channel_id=1, source_target_pairs={{6,0},{7,1},{4,2},{5,3},{10,4},{11,5},{8,6},{9,7},{14,8},{15,9},{1... | collective-permute-start | bytes 98312 | tf_op jit(solution)/shard_map/ppermute | solution.py:110
  68.1 0.6 collective-permute-start.25
  68.7 2.5 %collective-permute-start.24 = (f32[64,128]{1,0:T(8,128)S(1)}, f32[64,128]{1,0:T(8,128)S(1)}, u32[]{:S(2)}, u32[]{:S(2)}) collective-permute-start(f32[64,128]{1,0:T(8,128)S(1)} %get-tuple-element.47.refs_0_), channel_id=1, source_target_pairs={{3,0},{2,1},{1,2},{0,3},{7,4},{6,5},{5,6},{4,7},{11,8},{10,9},{9,1... | collective-permute-start | bytes 98312 | tf_op jit(solution)/shard_map/ppermute | solution.py:110
  71.4 1.1 collective-permute-done.25.refs_4_
  72.8 2.3 %collective-permute-done.23.refs_2_ = f32[64,128]{1,0:T(8,128)S(1)} collective-permute-done((f32[64,128]{1,0:T(8,128)S(1)}, f32[64,128]{1,0:T(8,128)S(1)}, u32[]{:S(2)}, u32[]{:S(2)}) %collective-permute-start.23) | collective-permute-done | bytes 32800 | tf_op jit(solution)/shard_map/ppermute | solution.py:110
  75.1 0.7 copy-done.9
  75.8 23.8 %shard_map.161 = (f32[1,64]{1,0:T(1,128)}, f32[8,16640]{1,0:T(8,128)S(1)}, f32[64,128]{1,0:T(8,128)S(1)}, f32[64,128]{1,0:T(8,128)S(1)}, f32[64,128]{1,0:T(8,128...) custom-call(f32[64,128]{1,0:T(8,128)S(1)} %get-tuple-element.47.refs, ...), custom_call_target="tpu_custom_call" | custom-call | tf_op jit(solution)/shard_map/pallas_call | solution.py:698
  99.6 5.2 %collective-permute-start.34 = (f32[64,128]{1,0:T(8,128)S(1)}, f32[64,128]{1,0:T(8,128)S(1)}, u32[]{:S(2)}, u32[]{:S(2)}) collective-permute-start(f32[64,128]{1,0:T(8,128)S(1)} %get-tuple-element.57), channel_id=1, source_target_pairs={{0,2},{1,3},{2,0},{3,1},{4,6},{5,7},{6,4},{7,5},{8,10},{9,11},{10,... | collective-permute-start | bytes 98312 | tf_op jit(solution)/shard_map/ppermute | solution.py:116
  104.8 1.2 collective-permute-start.36
  106.0 1.8 %collective-permute-start.37 = (f32[64,128]{1,0:T(8,128)S(1)}, f32[64,128]{1,0:T(8,128)S(1)}, u32[]{:S(2)}, u32[]{:S(2)}) collective-permute-start(f32[64,128]{1,0:T(8,128)S(1)} %get-tuple-element.60), channel_id=1, source_target_pairs={{0,5},{1,4},{2,7},{3,6},{4,9},{5,8},{6,11},{7,10},{8,13},{9,12},{1... | collective-permute-start | bytes 98312 | tf_op jit(solution)/shard_map/ppermute | solution.py:116
  108.0 2.1 %collective-permute-start.39 = (f32[64,128]{1,0:T(8,128)S(1)}, f32[64,128]{1,0:T(8,128)S(1)}, u32[]{:S(2)}, u32[]{:S(2)}) collective-permute-start(f32[64,128]{1,0:T(8,128)S(1)} %get-tuple-element.62), channel_id=1, source_target_pairs={{0,7},{1,6},{2,5},{3,4},{4,11},{5,10},{6,9},{7,8},{8,15},{9,14},{1... | collective-permute-start | bytes 98312 | tf_op jit(solution)/shard_map/ppermute | solution.py:116
  110.1 2.3 %collective-permute-start.40 = (f32[64,128]{1,0:T(8,128)S(1)}, f32[64,128]{1,0:T(8,128)S(1)}, u32[]{:S(2)}, u32[]{:S(2)}) collective-permute-start(f32[64,128]{1,0:T(8,128)S(1)} %get-tuple-element.63), channel_id=1, source_target_pairs={{0,12},{1,13},{2,14},{3,15},{4,0},{5,1},{6,2},{7,3},{8,4},{9,5},{1... | collective-permute-start | bytes 98312 | tf_op jit(solution)/shard_map/ppermute | solution.py:116
  112.4 1.6 %collective-permute-start.41 = (f32[64,128]{1,0:T(8,128)S(1)}, f32[64,128]{1,0:T(8,128)S(1)}, u32[]{:S(2)}, u32[]{:S(2)}) collective-permute-start(f32[64,128]{1,0:T(8,128)S(1)} %get-tuple-element.64), channel_id=1, source_target_pairs={{0,13},{1,12},{2,15},{3,14},{4,1},{5,0},{6,3},{7,2},{8,5},{9,4},{1... | collective-permute-start | bytes 98312 | tf_op jit(solution)/shard_map/ppermute | solution.py:116
  114.7 0.7 collective-permute-start.43
  115.7 3.3 %collective-permute-done.42.refs_10_ = f32[64,128]{1,0:T(8,128)S(1)} collective-permute-done((f32[64,128]{1,0:T(8,128)S(1)}, f32[64,128]{1,0:T(8,128)S(1)}, u32[]{:S(2)}, u32[]{:S(2)}) %collective-permute-start.42) | collective-permute-done | bytes 32800 | tf_op jit(solution)/shard_map/ppermute | solution.py:116
  119.3 14.8 %shard_map.162 = (f32[8,64]{1,0:T(8,128)S(1)}, f32[8,64]{1,0:T(8,128)S(1)}, f32[8,64]{1,0:T(8,128)S(1)}, f32[8,64]{1,0:T(8,128)S(1)}, f32[8,64]{1,0:T(8,128)S(1)...) custom-call(f32[64,128]{1,0:T(8,128)S(1)} %get-tuple-element.55.refs, ...), custom_call_target="tpu_custom_call" | custom-call | tf_op jit(solution)/shard_map/pallas_call | solution.py:698
  134.2 4.5 %collective-permute-start.45 = (f32[8,64]{1,0:T(8,128)S(1)}, f32[8,64]{1,0:T(8,128)S(1)}, u32[]{:S(2)}, u32[]{:S(2)}) collective-permute-start(f32[8,64]{1,0:T(8,128)S(1)} %get-tuple-element.72), channel_id=1, source_target_pairs={{0,2},{1,3},{2,0},{3,1},{4,6},{5,7},{6,4},{7,5},{8,10},{9,11},{10,... | collective-permute-start | bytes 6152 | tf_op jit(solution)/shard_map/ppermute | solution.py:116
  138.8 1.2 collective-permute-start.47
  140.5 1.4 collective-permute-start.49
  141.9 2.2 %collective-permute-start.50 = (f32[8,64]{1,0:T(8,128)S(1)}, f32[8,64]{1,0:T(8,128)S(1)}, u32[]{:S(2)}, u32[]{:S(2)}) collective-permute-start(f32[8,64]{1,0:T(8,128)S(1)} %get-tuple-element.77), channel_id=1, source_target_pairs={{0,7},{1,6},{2,5},{3,4},{4,11},{5,10},{6,9},{7,8},{8,15},{9,14},{1... | collective-permute-start | bytes 6152 | tf_op jit(solution)/shard_map/ppermute | solution.py:116
  144.1 1.4 collective-permute-start.51
  145.5 1.2 collective-permute-start.52
  146.7 1.6 %collective-permute-start.53 = (f32[8,64]{1,0:T(8,128)S(1)}, f32[8,64]{1,0:T(8,128)S(1)}, u32[]{:S(2)}, u32[]{:S(2)}) collective-permute-start(f32[8,64]{1,0:T(8,128)S(1)} %get-tuple-element.80), channel_id=1, source_target_pairs={{0,14},{1,15},{2,12},{3,13},{4,2},{5,3},{6,0},{7,1},{8,6},{9,7},{1... | collective-permute-start | bytes 6152 | tf_op jit(solution)/shard_map/ppermute | solution.py:116
  148.2 1.2 collective-permute-start.54
  149.4 1.8 %collective-permute-done.53 = f32[8,64]{1,0:T(8,128)S(1)} collective-permute-done((f32[8,64]{1,0:T(8,128)S(1)}, f32[8,64]{1,0:T(8,128)S(1)}, u32[]{:S(2)}, u32[]{:S(2)}) %collective-permute-start.53) | collective-permute-done | bytes 2080 | tf_op jit(solution)/shard_map/ppermute | solution.py:116
  151.2 1.0 collective-permute-done.54
  152.2 0.6 slice_add_fusion
  (82 shorter events, 5.8 us)
Async XLA Ops:
  0.6 42.3 %copy-start = (f32[2,384,128]{2,1,0:T(8,128)S(1)}, f32[2,384,128]{2,1,0:T(8,128)}, u32[]{:S(2)}) copy-start(f32[2,384,128]{2,1,0:T(8,128)} %refs_19_.1) | copy-start | bytes 1179652
  3.7 10.8 %collective-permute-start.10 = (f32[1,768]{1,0:T(1,128)S(1)}, f32[1,768]{1,0:T(1,128)S(1)}, u32[]{:S(2)}, u32[]{:S(2)}) collective-permute-start(f32[1,768]{1,0:T(1,128)S(1)} %convert_element_type.10.refs_0_), channel_id=1, source_target_pairs={{15,0},{14,1},{13,2},{12,3},{3,4},{2,5},{1,6},{0,7},{7,8},{6,9},{5... | collective-permute-start | bytes 9224 | tf_op jit(solution)/shard_map/ppermute | solution.py:110
  7.1 7.9 %collective-permute-start.9 = (f32[1,768]{1,0:T(1,128)S(1)}, f32[1,768]{1,0:T(1,128)S(1)}, u32[]{:S(2)}, u32[]{:S(2)}) collective-permute-start(f32[1,768]{1,0:T(1,128)S(1)} %convert_element_type.10.refs_0_), channel_id=1, source_target_pairs={{14,0},{15,1},{12,2},{13,3},{2,4},{3,5},{0,6},{1,7},{6,8},{7,9},{4... | collective-permute-start | bytes 9224 | tf_op jit(solution)/shard_map/ppermute | solution.py:110
  8.7 6.7 %collective-permute-start.8 = (f32[1,768]{1,0:T(1,128)S(1)}, f32[1,768]{1,0:T(1,128)S(1)}, u32[]{:S(2)}, u32[]{:S(2)}) collective-permute-start(f32[1,768]{1,0:T(1,128)S(1)} %convert_element_type.10.refs_0_), channel_id=1, source_target_pairs={{13,0},{12,1},{15,2},{14,3},{1,4},{0,5},{3,6},{2,7},{5,8},{4,9},{7... | collective-permute-start | bytes 9224 | tf_op jit(solution)/shard_map/ppermute | solution.py:110
  10.3 5.6 %collective-permute-start.7 = (f32[1,768]{1,0:T(1,128)S(1)}, f32[1,768]{1,0:T(1,128)S(1)}, u32[]{:S(2)}, u32[]{:S(2)}) collective-permute-start(f32[1,768]{1,0:T(1,128)S(1)} %convert_element_type.10.refs_0_), channel_id=1, source_target_pairs={{12,0},{13,1},{14,2},{15,3},{0,4},{1,5},{2,6},{3,7},{4,8},{5,9},{6... | collective-permute-start | bytes 9224 | tf_op jit(solution)/shard_map/ppermute | solution.py:110
  10.6 6.3 %collective-permute-start.6 = (f32[1,768]{1,0:T(1,128)S(1)}, f32[1,768]{1,0:T(1,128)S(1)}, u32[]{:S(2)}, u32[]{:S(2)}) collective-permute-start(f32[1,768]{1,0:T(1,128)S(1)} %convert_element_type.10.refs_0_), channel_id=1, source_target_pairs={{7,0},{6,1},{5,2},{4,3},{11,4},{10,5},{9,6},{8,7},{15,8},{14,9},{1... | collective-permute-start | bytes 9224 | tf_op jit(solution)/shard_map/ppermute | solution.py:110
  14.5 4.5 %collective-permute-start.5 = (f32[1,768]{1,0:T(1,128)S(1)}, f32[1,768]{1,0:T(1,128)S(1)}, u32[]{:S(2)}, u32[]{:S(2)}) collective-permute-start(f32[1,768]{1,0:T(1,128)S(1)} %convert_element_type.10.refs_0_), channel_id=1, source_target_pairs={{6,0},{7,1},{4,2},{5,3},{10,4},{11,5},{8,6},{9,7},{14,8},{15,9},{1... | collective-permute-start | bytes 9224 | tf_op jit(solution)/shard_map/ppermute | solution.py:110
  15.1 3.9 %collective-permute-start.4 = (f32[1,768]{1,0:T(1,128)S(1)}, f32[1,768]{1,0:T(1,128)S(1)}, u32[]{:S(2)}, u32[]{:S(2)}) collective-permute-start(f32[1,768]{1,0:T(1,128)S(1)} %convert_element_type.10.refs_0_), channel_id=1, source_target_pairs={{5,0},{4,1},{7,2},{6,3},{9,4},{8,5},{11,6},{10,7},{13,8},{12,9},{1... | collective-permute-start | bytes 9224 | tf_op jit(solution)/shard_map/ppermute | solution.py:110
  15.4 3.6 %collective-permute-start.3 = (f32[1,768]{1,0:T(1,128)S(1)}, f32[1,768]{1,0:T(1,128)S(1)}, u32[]{:S(2)}, u32[]{:S(2)}) collective-permute-start(f32[1,768]{1,0:T(1,128)S(1)} %convert_element_type.10.refs_0_), channel_id=1, source_target_pairs={{4,0},{5,1},{6,2},{7,3},{8,4},{9,5},{10,6},{11,7},{12,8},{13,9},{1... | collective-permute-start | bytes 9224 | tf_op jit(solution)/shard_map/ppermute | solution.py:110
  15.9 3.1 %collective-permute-start.2 = (f32[1,768]{1,0:T(1,128)S(1)}, f32[1,768]{1,0:T(1,128)S(1)}, u32[]{:S(2)}, u32[]{:S(2)}) collective-permute-start(f32[1,768]{1,0:T(1,128)S(1)} %convert_element_type.10.refs_0_), channel_id=1, source_target_pairs={{3,0},{2,1},{1,2},{0,3},{7,4},{6,5},{5,6},{4,7},{11,8},{10,9},{9,1... | collective-permute-start | bytes 9224 | tf_op jit(solution)/shard_map/ppermute | solution.py:110
  16.8 3.6 %collective-permute-start.1 = (f32[1,768]{1,0:T(1,128)S(1)}, f32[1,768]{1,0:T(1,128)S(1)}, u32[]{:S(2)}, u32[]{:S(2)}) collective-permute-start(f32[1,768]{1,0:T(1,128)S(1)} %convert_element_type.10.refs_0_), channel_id=1, source_target_pairs={{2,0},{3,1},{0,2},{1,3},{6,4},{7,5},{4,6},{5,7},{10,8},{11,9},{8,1... | collective-permute-start | bytes 9224 | tf_op jit(solution)/shard_map/ppermute | solution.py:110
  18.9 1.5 collective-permute-start
  20.4 0.7 copy-start.4
  21.2 0.7 copy-start.6
  21.9 0.7 copy-start.7
  22.5 0.7 copy-start.8
  25.9 8.0 %collective-permute-start.21 = (f32[8,1280]{1,0:T(8,128)S(1)}, f32[8,1280]{1,0:T(8,128)S(1)}, u32[]{:S(2)}, u32[]{:S(2)}) collective-permute-start(f32[8,1280]{1,0:T(8,128)S(1)} %get-tuple-element.43.refs_1_), channel_id=1, source_target_pairs={{15,0},{14,1},{13,2},{12,3},{3,4},{2,5},{1,6},{0,7},{7,8},{6,9},{5... | collective-permute-start | bytes 122888 | tf_op jit(solution)/shard_map/ppermute | solution.py:110
  26.7 8.5 %collective-permute-start.20 = (f32[8,1280]{1,0:T(8,128)S(1)}, f32[8,1280]{1,0:T(8,128)S(1)}, u32[]{:S(2)}, u32[]{:S(2)}) collective-permute-start(f32[8,1280]{1,0:T(8,128)S(1)} %get-tuple-element.43.refs_1_), channel_id=1, source_target_pairs={{14,0},{15,1},{12,2},{13,3},{2,4},{3,5},{0,6},{1,7},{6,8},{7,9},{4... | collective-permute-start | bytes 122888 | tf_op jit(solution)/shard_map/ppermute | solution.py:110
  29.0 6.9 %collective-permute-start.19 = (f32[8,1280]{1,0:T(8,128)S(1)}, f32[8,1280]{1,0:T(8,128)S(1)}, u32[]{:S(2)}, u32[]{:S(2)}) collective-permute-start(f32[8,1280]{1,0:T(8,128)S(1)} %get-tuple-element.43.refs_1_), channel_id=1, source_target_pairs={{13,0},{12,1},{15,2},{14,3},{1,4},{0,5},{3,6},{2,7},{5,8},{4,9},{7... | collective-permute-start | bytes 122888 | tf_op jit(solution)/shard_map/ppermute | solution.py:110
  30.9 6.2 %collective-permute-start.18 = (f32[8,1280]{1,0:T(8,128)S(1)}, f32[8,1280]{1,0:T(8,128)S(1)}, u32[]{:S(2)}, u32[]{:S(2)}) collective-permute-start(f32[8,1280]{1,0:T(8,128)S(1)} %get-tuple-element.43.refs_1_), channel_id=1, source_target_pairs={{12,0},{13,1},{14,2},{15,3},{0,4},{1,5},{2,6},{3,7},{4,8},{5,9},{6... | collective-permute-start | bytes 122888 | tf_op jit(solution)/shard_map/ppermute | solution.py:110
  31.2 5.9 %collective-permute-start.17 = (f32[8,1280]{1,0:T(8,128)S(1)}, f32[8,1280]{1,0:T(8,128)S(1)}, u32[]{:S(2)}, u32[]{:S(2)}) collective-permute-start(f32[8,1280]{1,0:T(8,128)S(1)} %get-tuple-element.43.refs_1_), channel_id=1, source_target_pairs={{7,0},{6,1},{5,2},{4,3},{11,4},{10,5},{9,6},{8,7},{15,8},{14,9},{1... | collective-permute-start | bytes 122888 | tf_op jit(solution)/shard_map/ppermute | solution.py:110
  33.9 5.0 %collective-permute-start.16 = (f32[8,1280]{1,0:T(8,128)S(1)}, f32[8,1280]{1,0:T(8,128)S(1)}, u32[]{:S(2)}, u32[]{:S(2)}) collective-permute-start(f32[8,1280]{1,0:T(8,128)S(1)} %get-tuple-element.43.refs_1_), channel_id=1, source_target_pairs={{6,0},{7,1},{4,2},{5,3},{10,4},{11,5},{8,6},{9,7},{14,8},{15,9},{1... | collective-permute-start | bytes 122888 | tf_op jit(solution)/shard_map/ppermute | solution.py:110
  35.2 7.6 %collective-permute-start.15 = (f32[8,1280]{1,0:T(8,128)S(1)}, f32[8,1280]{1,0:T(8,128)S(1)}, u32[]{:S(2)}, u32[]{:S(2)}) collective-permute-start(f32[8,1280]{1,0:T(8,128)S(1)} %get-tuple-element.43.refs_1_), channel_id=1, source_target_pairs={{5,0},{4,1},{7,2},{6,3},{9,4},{8,5},{11,6},{10,7},{13,8},{12,9},{1... | collective-permute-start | bytes 122888 | tf_op jit(solution)/shard_map/ppermute | solution.py:110
  36.0 6.9 %collective-permute-start.14 = (f32[8,1280]{1,0:T(8,128)S(1)}, f32[8,1280]{1,0:T(8,128)S(1)}, u32[]{:S(2)}, u32[]{:S(2)}) collective-permute-start(f32[8,1280]{1,0:T(8,128)S(1)} %get-tuple-element.43.refs_1_), channel_id=1, source_target_pairs={{4,0},{5,1},{6,2},{7,3},{8,4},{9,5},{10,6},{11,7},{12,8},{13,9},{1... | collective-permute-start | bytes 122888 | tf_op jit(solution)/shard_map/ppermute | solution.py:110
  37.1 5.8 %collective-permute-start.13 = (f32[8,1280]{1,0:T(8,128)S(1)}, f32[8,1280]{1,0:T(8,128)S(1)}, u32[]{:S(2)}, u32[]{:S(2)}) collective-permute-start(f32[8,1280]{1,0:T(8,128)S(1)} %get-tuple-element.43.refs_1_), channel_id=1, source_target_pairs={{3,0},{2,1},{1,2},{0,3},{7,4},{6,5},{5,6},{4,7},{11,8},{10,9},{9,1... | collective-permute-start | bytes 122888 | tf_op jit(solution)/shard_map/ppermute | solution.py:110
  37.1 5.8 %collective-permute-start.12 = (f32[8,1280]{1,0:T(8,128)S(1)}, f32[8,1280]{1,0:T(8,128)S(1)}, u32[]{:S(2)}, u32[]{:S(2)}) collective-permute-start(f32[8,1280]{1,0:T(8,128)S(1)} %get-tuple-element.43.refs_1_), channel_id=1, source_target_pairs={{2,0},{3,1},{0,2},{1,3},{6,4},{7,5},{4,6},{5,7},{10,8},{11,9},{8,1... | collective-permute-start | bytes 122888 | tf_op jit(solution)/shard_map/ppermute | solution.py:110
  38.9 4.0 %collective-permute-start.11 = (f32[8,1280]{1,0:T(8,128)S(1)}, f32[8,1280]{1,0:T(8,128)S(1)}, u32[]{:S(2)}, u32[]{:S(2)}) collective-permute-start(f32[8,1280]{1,0:T(8,128)S(1)} %get-tuple-element.43.refs_1_), channel_id=1, source_target_pairs={{1,0},{0,1},{3,2},{2,3},{5,4},{4,5},{7,6},{6,7},{9,8},{8,9},{11,10... | collective-permute-start | bytes 122888 | tf_op jit(solution)/shard_map/ppermute | solution.py:110
  39.8 0.9 copy-start.2
  40.7 0.8 copy-start.3
  41.6 0.7 copy-start.5
  43.6 0.9 copy-start.1
  56.8 9.0 %collective-permute-start.32 = (f32[64,128]{1,0:T(8,128)S(1)}, f32[64,128]{1,0:T(8,128)S(1)}, u32[]{:S(2)}, u32[]{:S(2)}) collective-permute-start(f32[64,128]{1,0:T(8,128)S(1)} %get-tuple-element.47.refs_0_), channel_id=1, source_target_pairs={{15,0},{14,1},{13,2},{12,3},{3,4},{2,5},{1,6},{0,7},{7,8},{6,9},{5... | collective-permute-start | bytes 98312 | tf_op jit(solution)/shard_map/ppermute | solution.py:110
  58.7 9.4 %collective-permute-start.31 = (f32[64,128]{1,0:T(8,128)S(1)}, f32[64,128]{1,0:T(8,128)S(1)}, u32[]{:S(2)}, u32[]{:S(2)}) collective-permute-start(f32[64,128]{1,0:T(8,128)S(1)} %get-tuple-element.47.refs_0_), channel_id=1, source_target_pairs={{14,0},{15,1},{12,2},{13,3},{2,4},{3,5},{0,6},{1,7},{6,8},{7,9},{4... | collective-permute-start | bytes 98312 | tf_op jit(solution)/shard_map/ppermute | solution.py:110
  61.9 6.2 %collective-permute-start.30 = (f32[64,128]{1,0:T(8,128)S(1)}, f32[64,128]{1,0:T(8,128)S(1)}, u32[]{:S(2)}, u32[]{:S(2)}) collective-permute-start(f32[64,128]{1,0:T(8,128)S(1)} %get-tuple-element.47.refs_0_), channel_id=1, source_target_pairs={{13,0},{12,1},{15,2},{14,3},{1,4},{0,5},{3,6},{2,7},{5,8},{4,9},{7... | collective-permute-start | bytes 98312 | tf_op jit(solution)/shard_map/ppermute | solution.py:110
  61.9 6.8 %collective-permute-start.29 = (f32[64,128]{1,0:T(8,128)S(1)}, f32[64,128]{1,0:T(8,128)S(1)}, u32[]{:S(2)}, u32[]{:S(2)}) collective-permute-start(f32[64,128]{1,0:T(8,128)S(1)} %get-tuple-element.47.refs_0_), channel_id=1, source_target_pairs={{12,0},{13,1},{14,2},{15,3},{0,4},{1,5},{2,6},{3,7},{4,8},{5,9},{6... | collective-permute-start | bytes 98312 | tf_op jit(solution)/shard_map/ppermute | solution.py:110
  62.2 9.0 %collective-permute-start.28 = (f32[64,128]{1,0:T(8,128)S(1)}, f32[64,128]{1,0:T(8,128)S(1)}, u32[]{:S(2)}, u32[]{:S(2)}) collective-permute-start(f32[64,128]{1,0:T(8,128)S(1)} %get-tuple-element.47.refs_0_), channel_id=1, source_target_pairs={{7,0},{6,1},{5,2},{4,3},{11,4},{10,5},{9,6},{8,7},{15,8},{14,9},{1... | collective-permute-start | bytes 98312 | tf_op jit(solution)/shard_map/ppermute | solution.py:110
  65.8 5.4 %collective-permute-start.27 = (f32[64,128]{1,0:T(8,128)S(1)}, f32[64,128]{1,0:T(8,128)S(1)}, u32[]{:S(2)}, u32[]{:S(2)}) collective-permute-start(f32[64,128]{1,0:T(8,128)S(1)} %get-tuple-element.47.refs_0_), channel_id=1, source_target_pairs={{6,0},{7,1},{4,2},{5,3},{10,4},{11,5},{8,6},{9,7},{14,8},{15,9},{1... | collective-permute-start | bytes 98312 | tf_op jit(solution)/shard_map/ppermute | solution.py:110
  68.1 3.3 %collective-permute-start.26 = (f32[64,128]{1,0:T(8,128)S(1)}, f32[64,128]{1,0:T(8,128)S(1)}, u32[]{:S(2)}, u32[]{:S(2)}) collective-permute-start(f32[64,128]{1,0:T(8,128)S(1)} %get-tuple-element.47.refs_0_), channel_id=1, source_target_pairs={{5,0},{4,1},{7,2},{6,3},{9,4},{8,5},{11,6},{10,7},{13,8},{12,9},{1... | collective-permute-start | bytes 98312 | tf_op jit(solution)/shard_map/ppermute | solution.py:110
  68.1 4.4 %collective-permute-start.25 = (f32[64,128]{1,0:T(8,128)S(1)}, f32[64,128]{1,0:T(8,128)S(1)}, u32[]{:S(2)}, u32[]{:S(2)}) collective-permute-start(f32[64,128]{1,0:T(8,128)S(1)} %get-tuple-element.47.refs_0_), channel_id=1, source_target_pairs={{4,0},{5,1},{6,2},{7,3},{8,4},{9,5},{10,6},{11,7},{12,8},{13,9},{1... | collective-permute-start | bytes 98312 | tf_op jit(solution)/shard_map/ppermute | solution.py:110
  68.7 4.1 %collective-permute-start.24 = (f32[64,128]{1,0:T(8,128)S(1)}, f32[64,128]{1,0:T(8,128)S(1)}, u32[]{:S(2)}, u32[]{:S(2)}) collective-permute-start(f32[64,128]{1,0:T(8,128)S(1)} %get-tuple-element.47.refs_0_), channel_id=1, source_target_pairs={{3,0},{2,1},{1,2},{0,3},{7,4},{6,5},{5,6},{4,7},{11,8},{10,9},{9,1... | collective-permute-start | bytes 98312 | tf_op jit(solution)/shard_map/ppermute | solution.py:110
  71.2 3.9 %collective-permute-start.23 = (f32[64,128]{1,0:T(8,128)S(1)}, f32[64,128]{1,0:T(8,128)S(1)}, u32[]{:S(2)}, u32[]{:S(2)}) collective-permute-start(f32[64,128]{1,0:T(8,128)S(1)} %get-tuple-element.47.refs_0_), channel_id=1, source_target_pairs={{2,0},{3,1},{0,2},{1,3},{6,4},{7,5},{4,6},{5,7},{10,8},{11,9},{8,1... | collective-permute-start | bytes 98312 | tf_op jit(solution)/shard_map/ppermute | solution.py:110
  71.2 3.9 %collective-permute-start.22 = (f32[64,128]{1,0:T(8,128)S(1)}, f32[64,128]{1,0:T(8,128)S(1)}, u32[]{:S(2)}, u32[]{:S(2)}) collective-permute-start(f32[64,128]{1,0:T(8,128)S(1)} %get-tuple-element.47.refs_0_), channel_id=1, source_target_pairs={{1,0},{0,1},{3,2},{2,3},{5,4},{4,5},{7,6},{6,7},{9,8},{8,9},{11,10... | collective-permute-start | bytes 98312 | tf_op jit(solution)/shard_map/ppermute | solution.py:110
  99.6 8.2 %collective-permute-start.33 = (f32[64,128]{1,0:T(8,128)S(1)}, f32[64,128]{1,0:T(8,128)S(1)}, u32[]{:S(2)}, u32[]{:S(2)}) collective-permute-start(f32[64,128]{1,0:T(8,128)S(1)} %get-tuple-element.56), channel_id=1, source_target_pairs={{0,1},{1,0},{2,3},{3,2},{4,5},{5,4},{6,7},{7,6},{8,9},{9,8},{10,11... | collective-permute-start | bytes 98312 | tf_op jit(solution)/shard_map/ppermute | solution.py:116
  99.6 8.4 %collective-permute-start.34 = (f32[64,128]{1,0:T(8,128)S(1)}, f32[64,128]{1,0:T(8,128)S(1)}, u32[]{:S(2)}, u32[]{:S(2)}) collective-permute-start(f32[64,128]{1,0:T(8,128)S(1)} %get-tuple-element.57), channel_id=1, source_target_pairs={{0,2},{1,3},{2,0},{3,1},{4,6},{5,7},{6,4},{7,5},{8,10},{9,11},{10,... | collective-permute-start | bytes 98312 | tf_op jit(solution)/shard_map/ppermute | solution.py:116
  104.8 5.3 %collective-permute-start.35 = (f32[64,128]{1,0:T(8,128)S(1)}, f32[64,128]{1,0:T(8,128)S(1)}, u32[]{:S(2)}, u32[]{:S(2)}) collective-permute-start(f32[64,128]{1,0:T(8,128)S(1)} %get-tuple-element.58), channel_id=1, source_target_pairs={{0,3},{1,2},{2,1},{3,0},{4,7},{5,6},{6,5},{7,4},{8,11},{9,10},{10,... | collective-permute-start | bytes 98312 | tf_op jit(solution)/shard_map/ppermute | solution.py:116
  104.8 7.6 %collective-permute-start.36 = (f32[64,128]{1,0:T(8,128)S(1)}, f32[64,128]{1,0:T(8,128)S(1)}, u32[]{:S(2)}, u32[]{:S(2)}) collective-permute-start(f32[64,128]{1,0:T(8,128)S(1)} %get-tuple-element.59), channel_id=1, source_target_pairs={{0,4},{1,5},{2,6},{3,7},{4,8},{5,9},{6,10},{7,11},{8,12},{9,13},{1... | collective-permute-start | bytes 98312 | tf_op jit(solution)/shard_map/ppermute | solution.py:116
  106.0 8.0 %collective-permute-start.37 = (f32[64,128]{1,0:T(8,128)S(1)}, f32[64,128]{1,0:T(8,128)S(1)}, u32[]{:S(2)}, u32[]{:S(2)}) collective-permute-start(f32[64,128]{1,0:T(8,128)S(1)} %get-tuple-element.60), channel_id=1, source_target_pairs={{0,5},{1,4},{2,7},{3,6},{4,9},{5,8},{6,11},{7,10},{8,13},{9,12},{1... | collective-permute-start | bytes 98312 | tf_op jit(solution)/shard_map/ppermute | solution.py:116
  107.8 6.9 %collective-permute-start.38 = (f32[64,128]{1,0:T(8,128)S(1)}, f32[64,128]{1,0:T(8,128)S(1)}, u32[]{:S(2)}, u32[]{:S(2)}) collective-permute-start(f32[64,128]{1,0:T(8,128)S(1)} %get-tuple-element.61), channel_id=1, source_target_pairs={{0,6},{1,7},{2,4},{3,5},{4,10},{5,11},{6,8},{7,9},{8,14},{9,15},{1... | collective-permute-start | bytes 98312 | tf_op jit(solution)/shard_map/ppermute | solution.py:116
  108.0 7.4 %collective-permute-start.39 = (f32[64,128]{1,0:T(8,128)S(1)}, f32[64,128]{1,0:T(8,128)S(1)}, u32[]{:S(2)}, u32[]{:S(2)}) collective-permute-start(f32[64,128]{1,0:T(8,128)S(1)} %get-tuple-element.62), channel_id=1, source_target_pairs={{0,7},{1,6},{2,5},{3,4},{4,11},{5,10},{6,9},{7,8},{8,15},{9,14},{1... | collective-permute-start | bytes 98312 | tf_op jit(solution)/shard_map/ppermute | solution.py:116
  110.1 5.3 %collective-permute-start.40 = (f32[64,128]{1,0:T(8,128)S(1)}, f32[64,128]{1,0:T(8,128)S(1)}, u32[]{:S(2)}, u32[]{:S(2)}) collective-permute-start(f32[64,128]{1,0:T(8,128)S(1)} %get-tuple-element.63), channel_id=1, source_target_pairs={{0,12},{1,13},{2,14},{3,15},{4,0},{5,1},{6,2},{7,3},{8,4},{9,5},{1... | collective-permute-start | bytes 98312 | tf_op jit(solution)/shard_map/ppermute | solution.py:116
  112.4 3.4 %collective-permute-start.41 = (f32[64,128]{1,0:T(8,128)S(1)}, f32[64,128]{1,0:T(8,128)S(1)}, u32[]{:S(2)}, u32[]{:S(2)}) collective-permute-start(f32[64,128]{1,0:T(8,128)S(1)} %get-tuple-element.64), channel_id=1, source_target_pairs={{0,13},{1,12},{2,15},{3,14},{4,1},{5,0},{6,3},{7,2},{8,5},{9,4},{1... | collective-permute-start | bytes 98312 | tf_op jit(solution)/shard_map/ppermute | solution.py:116
  114.0 5.0 %collective-permute-start.42 = (f32[64,128]{1,0:T(8,128)S(1)}, f32[64,128]{1,0:T(8,128)S(1)}, u32[]{:S(2)}, u32[]{:S(2)}) collective-permute-start(f32[64,128]{1,0:T(8,128)S(1)} %get-tuple-element.65), channel_id=1, source_target_pairs={{0,14},{1,15},{2,12},{3,13},{4,2},{5,3},{6,0},{7,1},{8,6},{9,7},{1... | collective-permute-start | bytes 98312 | tf_op jit(solution)/shard_map/ppermute | solution.py:116
  114.7 4.6 %collective-permute-start.43 = (f32[64,128]{1,0:T(8,128)S(1)}, f32[64,128]{1,0:T(8,128)S(1)}, u32[]{:S(2)}, u32[]{:S(2)}) collective-permute-start(f32[64,128]{1,0:T(8,128)S(1)} %get-tuple-element.66), channel_id=1, source_target_pairs={{0,15},{1,14},{2,13},{3,12},{4,3},{5,2},{6,1},{7,0},{8,7},{9,6},{1... | collective-permute-start | bytes 98312 | tf_op jit(solution)/shard_map/ppermute | solution.py:116
  134.1 6.4 %collective-permute-start.44 = (f32[8,64]{1,0:T(8,128)S(1)}, f32[8,64]{1,0:T(8,128)S(1)}, u32[]{:S(2)}, u32[]{:S(2)}) collective-permute-start(f32[8,64]{1,0:T(8,128)S(1)} %get-tuple-element.71), channel_id=1, source_target_pairs={{0,1},{1,0},{2,3},{3,2},{4,5},{5,4},{6,7},{7,6},{8,9},{9,8},{10,11... | collective-permute-start | bytes 6152 | tf_op jit(solution)/shard_map/ppermute | solution.py:116
  134.2 7.7 %collective-permute-start.45 = (f32[8,64]{1,0:T(8,128)S(1)}, f32[8,64]{1,0:T(8,128)S(1)}, u32[]{:S(2)}, u32[]{:S(2)}) collective-permute-start(f32[8,64]{1,0:T(8,128)S(1)} %get-tuple-element.72), channel_id=1, source_target_pairs={{0,2},{1,3},{2,0},{3,1},{4,6},{5,7},{6,4},{7,5},{8,10},{9,11},{10,... | collective-permute-start | bytes 6152 | tf_op jit(solution)/shard_map/ppermute | solution.py:116
  138.8 5.3 %collective-permute-start.46 = (f32[8,64]{1,0:T(8,128)S(1)}, f32[8,64]{1,0:T(8,128)S(1)}, u32[]{:S(2)}, u32[]{:S(2)}) collective-permute-start(f32[8,64]{1,0:T(8,128)S(1)} %get-tuple-element.73), channel_id=1, source_target_pairs={{0,3},{1,2},{2,1},{3,0},{4,7},{5,6},{6,5},{7,4},{8,11},{9,10},{10,... | collective-permute-start | bytes 6152 | tf_op jit(solution)/shard_map/ppermute | solution.py:116
  138.8 6.7 %collective-permute-start.47 = (f32[8,64]{1,0:T(8,128)S(1)}, f32[8,64]{1,0:T(8,128)S(1)}, u32[]{:S(2)}, u32[]{:S(2)}) collective-permute-start(f32[8,64]{1,0:T(8,128)S(1)} %get-tuple-element.74), channel_id=1, source_target_pairs={{0,4},{1,5},{2,6},{3,7},{4,8},{5,9},{6,10},{7,11},{8,12},{9,13},{1... | collective-permute-start | bytes 6152 | tf_op jit(solution)/shard_map/ppermute | solution.py:116
  140.0 6.7 %collective-permute-start.48 = (f32[8,64]{1,0:T(8,128)S(1)}, f32[8,64]{1,0:T(8,128)S(1)}, u32[]{:S(2)}, u32[]{:S(2)}) collective-permute-start(f32[8,64]{1,0:T(8,128)S(1)} %get-tuple-element.75), channel_id=1, source_target_pairs={{0,5},{1,4},{2,7},{3,6},{4,9},{5,8},{6,11},{7,10},{8,13},{9,12},{1... | collective-permute-start | bytes 6152 | tf_op jit(solution)/shard_map/ppermute | solution.py:116
  140.5 7.8 %collective-permute-start.49 = (f32[8,64]{1,0:T(8,128)S(1)}, f32[8,64]{1,0:T(8,128)S(1)}, u32[]{:S(2)}, u32[]{:S(2)}) collective-permute-start(f32[8,64]{1,0:T(8,128)S(1)} %get-tuple-element.76), channel_id=1, source_target_pairs={{0,6},{1,7},{2,4},{3,5},{4,10},{5,11},{6,8},{7,9},{8,14},{9,15},{1... | collective-permute-start | bytes 6152 | tf_op jit(solution)/shard_map/ppermute | solution.py:116
  141.9 7.5 %collective-permute-start.50 = (f32[8,64]{1,0:T(8,128)S(1)}, f32[8,64]{1,0:T(8,128)S(1)}, u32[]{:S(2)}, u32[]{:S(2)}) collective-permute-start(f32[8,64]{1,0:T(8,128)S(1)} %get-tuple-element.77), channel_id=1, source_target_pairs={{0,7},{1,6},{2,5},{3,4},{4,11},{5,10},{6,9},{7,8},{8,15},{9,14},{1... | collective-permute-start | bytes 6152 | tf_op jit(solution)/shard_map/ppermute | solution.py:116
  144.1 5.3 %collective-permute-start.51 = (f32[8,64]{1,0:T(8,128)S(1)}, f32[8,64]{1,0:T(8,128)S(1)}, u32[]{:S(2)}, u32[]{:S(2)}) collective-permute-start(f32[8,64]{1,0:T(8,128)S(1)} %get-tuple-element.78), channel_id=1, source_target_pairs={{0,12},{1,13},{2,14},{3,15},{4,0},{5,1},{6,2},{7,3},{8,4},{9,5},{1... | collective-permute-start | bytes 6152 | tf_op jit(solution)/shard_map/ppermute | solution.py:116
  145.5 3.9 %collective-permute-start.52 = (f32[8,64]{1,0:T(8,128)S(1)}, f32[8,64]{1,0:T(8,128)S(1)}, u32[]{:S(2)}, u32[]{:S(2)}) collective-permute-start(f32[8,64]{1,0:T(8,128)S(1)} %get-tuple-element.79), channel_id=1, source_target_pairs={{0,13},{1,12},{2,15},{3,14},{4,1},{5,0},{6,3},{7,2},{8,5},{9,4},{1... | collective-permute-start | bytes 6152 | tf_op jit(solution)/shard_map/ppermute | solution.py:116
  146.7 4.5 %collective-permute-start.53 = (f32[8,64]{1,0:T(8,128)S(1)}, f32[8,64]{1,0:T(8,128)S(1)}, u32[]{:S(2)}, u32[]{:S(2)}) collective-permute-start(f32[8,64]{1,0:T(8,128)S(1)} %get-tuple-element.80), channel_id=1, source_target_pairs={{0,14},{1,15},{2,12},{3,13},{4,2},{5,3},{6,0},{7,1},{8,6},{9,7},{1... | collective-permute-start | bytes 6152 | tf_op jit(solution)/shard_map/ppermute | solution.py:116
  148.2 3.9 %collective-permute-start.54 = (f32[8,64]{1,0:T(8,128)S(1)}, f32[8,64]{1,0:T(8,128)S(1)}, u32[]{:S(2)}, u32[]{:S(2)}) collective-permute-start(f32[8,64]{1,0:T(8,128)S(1)} %get-tuple-element.81), channel_id=1, source_target_pairs={{0,15},{1,14},{2,13},{3,12},{4,3},{5,2},{6,1},{7,0},{8,7},{9,6},{1... | collective-permute-start | bytes 6152 | tf_op jit(solution)/shard_map/ppermute | solution.py:116
  (2 other events, 1.4 us)
